TPU v7x, 32 devices: a whole 2x2x4 slice. The times are simulated.
32 devices in a mesh: dp: 4 (over y, x), expert: 8 (over z, core).
Axes of the slice: x: 2, y: 2, z: 4, core: 2. Of those that a mesh axis runs over, the one named last changes fastest.
Arguments:
- tokens: bfloat16 [8, 4, 12, 7168], P('expert', 'dp'), may hold values from -6 to 6
- cotangent: bfloat16 [8, 4, 12, 7168], P('expert', 'dp'), may hold values from -6 to 6
- w_gate: bfloat16 [8, 7168, 1024], P('expert', None, 'dp'), may hold values from -0.0625 to 0.0625
- w_up: bfloat16 [8, 7168, 1024], P('expert', None, 'dp'), may hold values from -0.0625 to 0.0625
- w_down: bfloat16 [8, 1024, 7168], P('expert', 'dp'), may hold values from -0.1875 to 0.1875
- routes: int32 [8, 4, 12, 2], P('expert', 'dp'), may hold values from 0 to 7, all different within a row; in each aligned block of 48 rows (0 to 47, 48 to 95, ..., all dimensions but the last counted through in order) at most 18 rows name the same one
- gates: int32 [8, 4, 12, 2], P('expert', 'dp'), may hold values from 4096 to 65535
- matching: int32 [8], replicated, may hold values from 0 to 7, as said below
Outputs:
- grad_input: bfloat16 [8, 4, 12, 7168], P('expert', 'dp')
- grad_gate: bfloat16 [8, 7168, 1024], P('expert', None, 'dp')
- grad_up: bfloat16 [8, 7168, 1024], P('expert', None, 'dp')
- grad_down: bfloat16 [8, 1024, 7168], P('expert', 'dp')
Inputs may be any that keep to these rules, and one draw needn't show every extreme that they name: Each token names 2 different experts. Within routes[c] for any c no expert is named more than 18 times. matching[j] is j, or j + 4 for j below 4, or j - 4 above; matching[matching[j]] = j, and the pair of slot 7 always differs from it.
All inputs are finite; a program needn't handle non-finite values.
Results may differ from a plain program's by a relative error of at most 0.019.
Values may be sent and summed in bfloat16 or wider, within the bound.
A program may use at most 192 MiB of HBM per device.

v0:
```python
import jax
import jax.numpy as jnp
from jax import lax
from jax.sharding import PartitionSpec as P


def from_partner(x, axis, distance):
    return lax.ppermute(x, axis, [(i, i ^ 1 << distance) for i in range(lax.axis_size(axis))])


def column_places(route_flat, owner_table, expert_count, cap_col):
    choices_iota = jnp.arange(expert_count, dtype=jnp.int32)
    onehot = (route_flat[:, None] == choices_iota[None, :]).astype(jnp.int32)
    ranking = jnp.sum(jnp.cumsum(onehot, axis=0) * onehot, axis=1) - 1
    target = jnp.sum(onehot * owner_table[None, :], axis=1)
    position = target * cap_col + ranking
    slot_iota = jnp.arange(expert_count * cap_col, dtype=jnp.int32)
    return slot_iota[:, None] == position[None, :]


def contract_rows(left, right):
    return lax.dot_general(
        left, right, (((0,), (0,)), ((), ())), preferred_element_type=jnp.float32
    )


def contract_units(left, right):
    return lax.dot_general(
        left, right, (((1,), (1,)), ((), ())), preferred_element_type=jnp.float32
    )


def shards(tokens, cotangent, w_gate, w_up, w_down, routes, gates, matching):
    rows_here = tokens.shape[2]
    width = tokens.shape[3]
    topk = routes.shape[3]
    expert_count = lax.axis_size("expert")
    group_count = lax.axis_size("dp")
    cap_col = 3 * group_count * rows_here * topk // (2 * expert_count)
    slot_count = expert_count * cap_col
    column_tok = group_count * rows_here
    self_index = lax.axis_index("expert")
    pair_bit = expert_count.bit_length() - 2
    expert_iota = jnp.arange(expert_count, dtype=jnp.int32)
    partner = jnp.sum(jnp.where(expert_iota == self_index, matching, 0))
    flipped = partner != self_index
    weight_gate = w_gate[0]
    weight_up = w_up[0]
    weight_down = w_down[0]
    swapped = from_partner((weight_gate, weight_up, weight_down), "expert", pair_bit)
    weight_gate = jnp.where(flipped, swapped[0], weight_gate)
    weight_up = jnp.where(flipped, swapped[1], weight_up)
    weight_down = jnp.where(flipped, swapped[2], weight_down)
    labels = (
        lax.all_gather(routes, "dp", axis=1, tiled=True),
        lax.all_gather(gates, "dp", axis=1, tiled=True),
    )
    route_col = labels[0].reshape(column_tok * topk)
    gate_col = labels[1].reshape(column_tok, topk).astype(jnp.float32) / 65536.0
    places = column_places(route_col, matching, expert_count, cap_col)
    place_pick = places.astype(jnp.bfloat16)
    place_tok = jnp.any(places.reshape(slot_count, column_tok, topk), axis=2).astype(jnp.bfloat16)
    column = (
        lax.all_gather(tokens, "dp", axis=1, tiled=True),
        lax.all_gather(cotangent, "dp", axis=1, tiled=True),
    )
    col_in = column[0].reshape(column_tok, width)
    col_cot = column[1].reshape(column_tok, width)
    send_in = jnp.dot(place_tok, col_in, preferred_element_type=jnp.float32).astype(jnp.bfloat16)
    dy_pick = (gate_col[:, :, None] * col_cot[:, None, :].astype(jnp.float32)).astype(jnp.bfloat16)
    send_cot = jnp.dot(
        place_pick, dy_pick.reshape(column_tok * topk, width), preferred_element_type=jnp.float32
    ).astype(jnp.bfloat16)
    arrived = (
        lax.all_to_all(
            send_in.reshape(expert_count, cap_col, width),
            "expert",
            split_axis=0,
            concat_axis=0,
            tiled=True,
        ),
        lax.all_to_all(
            send_cot.reshape(expert_count, cap_col, width),
            "expert",
            split_axis=0,
            concat_axis=0,
            tiled=True,
        ),
    )
    routed_rows = arrived[0].reshape(slot_count, width)
    routed_cot = arrived[1].reshape(slot_count, width)
    gate_act = jnp.dot(routed_rows, weight_gate, preferred_element_type=jnp.float32)
    up_act = jnp.dot(routed_rows, weight_up, preferred_element_type=jnp.float32)
    sigmoid_gate = jax.nn.sigmoid(gate_act)
    hidden = (gate_act * sigmoid_gate * up_act).astype(jnp.bfloat16)
    grad_down_here = contract_rows(hidden, routed_cot).astype(jnp.bfloat16)
    d_hidden = contract_units(routed_cot, weight_down)
    d_gate = (d_hidden * up_act * sigmoid_gate * (1.0 + gate_act * (1.0 - sigmoid_gate))).astype(
        jnp.bfloat16
    )
    d_up = (d_hidden * gate_act * sigmoid_gate).astype(jnp.bfloat16)
    grad_gate_here = contract_rows(routed_rows, d_gate).astype(jnp.bfloat16)
    grad_up_here = contract_rows(routed_rows, d_up).astype(jnp.bfloat16)
    partial_terms = contract_units(d_gate, weight_gate) + contract_units(d_up, weight_up)
    parts = partial_terms.astype(jnp.bfloat16).reshape(expert_count, cap_col, width)
    back = lax.all_to_all(parts, "expert", split_axis=0, concat_axis=0, tiled=True)
    col_sum = contract_rows(place_tok, back.reshape(slot_count, width))
    total = lax.psum_scatter(
        col_sum.reshape(group_count, rows_here, width).astype(jnp.bfloat16),
        "dp",
        scatter_dimension=0,
        tiled=True,
    )
    return (
        total.reshape(1, 1, rows_here, width),
        grad_gate_here[None],
        grad_up_here[None],
        grad_down_here[None],
    )


def solution(mesh):
    placed = (
        P("expert", "dp", None, None),
        P("expert", "dp", None, None),
        P("expert", None, "dp"),
        P("expert", None, "dp"),
        P("expert", "dp", None),
        P("expert", "dp", None, None),
        P("expert", "dp", None, None),
        P(),
    )
    return jax.shard_map(
        shards,
        mesh=mesh,
        in_specs=placed,
        out_specs=(
            P("expert", "dp", None, None),
            P("expert", None, "dp"),
            P("expert", None, "dp"),
            P("expert", "dp", None),
        ),
        check_vma=False,
    )
```

profile of v0, /device:TPU:0, one launch (start us, length us, event | category | flops | bytes accessed | tf_op | source)
XLA Modules:
  0.0 747.7 jit_solution(13272461907656189469)
XLA Ops:
  7.2 9.6 %all_gather.12 = s32[1,4,12,2]{2,3,0,1:T(2,128)S(1)} all-gather(s32[1,1,12,2]{2,3,0,1:T(2,128)} %bitcast.61), channel_id=1, replica_groups=mesh['dp'=4,'expert'=8] {'dp'}, dimensions={1}, use_global_device_ids=true | all-gather | bytes 480 | tf_op jit(solution)/shard_map/all_gather | solution.py:55
  18.4 12.7 %all_gather.15 = bf16[1,4,12,7168]{3,2,0,1:T(8,128)(2,1)S(1)} all-gather(bf16[1,1,12,7168]{3,2,0,1:T(8,128)(2,1)} %bitcast.58), channel_id=1, replica_groups=mesh['dp'=4,'expert'=8] {'dp'}, dimensions={1}, use_global_device_ids=true | all-gather | bytes 860160 | tf_op jit(solution)/shard_map/all_gather | solution.py:64
  32.0 1.9 reshape.85
  34.0 5.0 all-to-all-start.1
  39.0 2.9 collective-permute-start.1
  41.9 12.6 %all_gather.14 = bf16[1,4,12,7168]{3,2,0,1:T(8,128)(2,1)} all-gather(bf16[1,1,12,7168]{3,2,0,1:T(8,128)(2,1)S(1)} %bitcast.59), channel_id=1, replica_groups=mesh['dp'=4,'expert'=8] {'dp'}, dimensions={1}, use_global_device_ids=true | all-gather | bytes 860160 | tf_op jit(solution)/shard_map/all_gather | solution.py:65
  54.5 2.4 reshape.90
  56.9 3.8 mul.69
  60.7 4.5 mul.70
  65.3 7.6 %all_gather.13 = s32[1,4,12,2]{2,3,0,1:T(2,128)S(1)} all-gather(s32[1,1,12,2]{2,3,0,1:T(2,128)S(1)} %bitcast.62), channel_id=1, replica_groups=mesh['dp'=4,'expert'=8] {'dp'}, dimensions={1}, use_global_device_ids=true | all-gather | bytes 480 | tf_op jit(solution)/shard_map/all_gather | solution.py:56
  73.1 3.9 convolution_convert_fusion.4
  77.0 3.1 reshape.82
  80.1 101.1 %all-to-all-done.1 = bf16[8,18,7168]{2,1,0:T(8,128)(2,1)S(1)} async-done(((bf16[8,18,7168]{2,1,0:T(8,128)(2,1)}), bf16[8,18,7168]{2,1,0:T(8,128)(2,1)S(1)}, u32[]{:S(2)}, u32[]{:S(2)}) %all-to-all-start.1) | async-done | bytes 2064416 | tf_op jit(solution)/shard_map/all_to_all | solution.py:75
  181.2 4.4 all-to-all-start
  185.6 2.8 collective-permute-start.2
  189.9 1.7 reshape.86
  191.6 284.7 %all-to-all-done = bf16[8,18,7168]{2,1,0:T(8,128)(2,1)} async-done(((bf16[8,18,7168]{2,1,0:T(8,128)(2,1)}), bf16[8,18,7168]{2,1,0:T(8,128)(2,1)}, u32[]{:S(2)}, u32[]{:S(2)}) %all-to-all-start) | async-done | bytes 2064416 | tf_op jit(solution)/shard_map/all_to_all | solution.py:82
  476.3 2.1 reshape.83
  478.5 4.1 fusion.8
  482.7 72.3 %collective-permute-done.2 = bf16[7168,256]{1,0:T(8,128)(2,1)} collective-permute-done((bf16[7168,256]{1,0:T(8,128)(2,1)}, bf16[7168,256]{1,0:T(8,128)(2,1)}, u32[]{:S(2)}, u32[]{:S(2)}) %collective-permute-start.2) | collective-permute-done | bytes 3670048 | tf_op jit(solution)/shard_map/ppermute | solution.py:8
  555.9 77.2 %collective-permute-done = bf16[256,7168]{1,0:T(8,128)(2,1)} collective-permute-done((bf16[256,7168]{1,0:T(8,128)(2,1)}, bf16[256,7168]{1,0:T(8,128)(2,1)}, u32[]{:S(2)}, u32[]{:S(2)}) %collective-permute-start) | collective-permute-done | bytes 3670048 | tf_op jit(solution)/shard_map/ppermute | solution.py:8
  634.3 1.4 fusion.7
  635.7 1.6 fusion.3
  637.3 1.9 reshape.87
  639.2 8.6 %all-to-all-start.2 = ((bf16[8,18,7168]{2,1,0:T(8,128)(2,1)}), bf16[8,18,7168]{2,1,0:T(8,128)(2,1)S(1)}, u32[]{:S(2)}, u32[]{:S(2)}) async-start(bf16[8,18,7168]{2,1,0:T(8,128)(2,1)} %reshape.87), calls=%async_computation.2 | async-start | bytes 5505024 | tf_op jit(solution)/shard_map/all_to_all | solution.py:106
  647.9 63.0 %all-to-all-done.2 = bf16[8,18,7168]{2,1,0:T(8,128)(2,1)S(1)} async-done(((bf16[8,18,7168]{2,1,0:T(8,128)(2,1)}), bf16[8,18,7168]{2,1,0:T(8,128)(2,1)S(1)}, u32[]{:S(2)}, u32[]{:S(2)}) %all-to-all-start.2) | async-done | bytes 2064416 | tf_op jit(solution)/shard_map/all_to_all | solution.py:106
  710.9 1.7 reshape.91
  712.6 3.1 convolution_convert_fusion.5
  715.8 3.0 fusion.2
  718.8 3.1 fusion
  721.9 3.1 fusion.1
  724.9 16.0 %reduce-scatter.4.cloned.1.call-done = bf16[1,12,7168]{2,1,0:T(8,128)(2,1)} async-done(((bf16[4,12,7168]{2,1,0:T(8,128)(2,1)}), bf16[1,12,7168]{2,1,0:T(8,128)(2,1)}) %reduce-scatter.4.cloned.1.call-update) | async-done | bytes 172048
  (42 shorter events, 5.8 us)
Async XLA Ops:
  34.0 7.9 %copy-start.6 = (bf16[1,1,12,7168]{3,2,1,0:T(8,128)(2,1)S(1)}, bf16[1,1,12,7168]{3,2,1,0:T(8,128)(2,1)}, u32[]{:S(2)}) copy-start(bf16[1,1,12,7168]{3,2,1,0:T(8,128)(2,1)} %param.9) | copy-start | bytes 516100
  34.0 147.2 %all-to-all-start.1 = ((bf16[8,18,7168]{2,1,0:T(8,128)(2,1)}), bf16[8,18,7168]{2,1,0:T(8,128)(2,1)S(1)}, u32[]{:S(2)}, u32[]{:S(2)}) async-start(bf16[8,18,7168]{2,1,0:T(8,128)(2,1)} %reshape.85), calls=%async_computation.1 | async-start | bytes 5505024 | tf_op jit(solution)/shard_map/all_to_all | solution.py:75
  39.0 439.5 %collective-permute-start.1 = (bf16[7168,256]{1,0:T(8,128)(2,1)}, bf16[7168,256]{1,0:T(8,128)(2,1)}, u32[]{:S(2)}, u32[]{:S(2)}) collective-permute-start(bf16[7168,256]{1,0:T(8,128)(2,1)} %bitcast.56), channel_id=1, source_target_pairs={{0,4},{1,5},{2,6},{3,7},{4,0},{5,1},{6,2},{7,3},{8,12},{9,13},{10,... | collective-permute-start | bytes 11010056 | tf_op jit(solution)/shard_map/ppermute | solution.py:8
  60.7 4.5 copy-start.7
  80.1 108.6 %copy-start.8 = (s32[8]{0:T(128)S(1)}, s32[8]{0:T(128)}, u32[]{:S(2)}) copy-start(s32[8]{0:T(128)} %param.15) | copy-start | bytes 100
  181.2 295.1 %all-to-all-start = ((bf16[8,18,7168]{2,1,0:T(8,128)(2,1)}), bf16[8,18,7168]{2,1,0:T(8,128)(2,1)}, u32[]{:S(2)}, u32[]{:S(2)}) async-start(bf16[8,18,7168]{2,1,0:T(8,128)(2,1)} %reshape.82), calls=%async_computation | async-start | bytes 5505024 | tf_op jit(solution)/shard_map/all_to_all | solution.py:82
  185.6 369.3 %collective-permute-start.2 = (bf16[7168,256]{1,0:T(8,128)(2,1)}, bf16[7168,256]{1,0:T(8,128)(2,1)}, u32[]{:S(2)}, u32[]{:S(2)}) collective-permute-start(bf16[7168,256]{1,0:T(8,128)(2,1)} %bitcast.57), channel_id=1, source_target_pairs={{0,4},{1,5},{2,6},{3,7},{4,0},{5,1},{6,2},{7,3},{8,12},{9,13},{10,... | collective-permute-start | bytes 11010056 | tf_op jit(solution)/shard_map/ppermute | solution.py:8
  188.5 444.7 %collective-permute-start = (bf16[256,7168]{1,0:T(8,128)(2,1)}, bf16[256,7168]{1,0:T(8,128)(2,1)}, u32[]{:S(2)}, u32[]{:S(2)}) collective-permute-start(bf16[256,7168]{1,0:T(8,128)(2,1)} %bitcast.63), channel_id=1, source_target_pairs={{0,4},{1,5},{2,6},{3,7},{4,0},{5,1},{6,2},{7,3},{8,12},{9,13},{10,... | collective-permute-start | bytes 11010056 | tf_op jit(solution)/shard_map/ppermute | solution.py:8
  478.4 154.7 %copy-start = (bf16[144,7168]{1,0:T(8,128)(2,1)}, bf16[144,7168]{1,0:T(8,128)(2,1)S(1)}, u32[]{:S(2)}) copy-start(bf16[144,7168]{1,0:T(8,128)(2,1)S(1)} %reshape.83) | copy-start | bytes 6193156
  478.5 76.5 %copy-start.3 = (bf16[1,7168,256]{2,1,0:T(8,128)(2,1)S(1)}, bf16[1,7168,256]{2,1,0:T(8,128)(2,1)}, u32[]{:S(2)}) copy-start(bf16[1,7168,256]{2,1,0:T(8,128)(2,1)} %param.10) | copy-start | bytes 11010052
  478.5 76.5 %copy-start.4 = (bf16[144,7168]{1,0:T(8,128)(2,1)S(1)}, bf16[144,7168]{1,0:T(8,128)(2,1)}, u32[]{:S(2)}) copy-start(bf16[144,7168]{1,0:T(8,128)(2,1)} %reshape.86) | copy-start | bytes 6193156
  482.6 150.5 %copy-start.9 = (bf16[1,256,7168]{2,1,0:T(8,128)(2,1)S(1)}, bf16[1,256,7168]{2,1,0:T(8,128)(2,1)}, u32[]{:S(2)}) copy-start(bf16[1,256,7168]{2,1,0:T(8,128)(2,1)} %param.12) | copy-start | bytes 11010052
  555.9 78.4 %copy-start.2 = (bf16[1,7168,256]{2,1,0:T(8,128)(2,1)S(1)}, bf16[1,7168,256]{2,1,0:T(8,128)(2,1)}, u32[]{:S(2)}) copy-start(bf16[1,7168,256]{2,1,0:T(8,128)(2,1)} %param.11) | copy-start | bytes 11010052
  639.2 71.7 %all-to-all-start.2 = ((bf16[8,18,7168]{2,1,0:T(8,128)(2,1)}), bf16[8,18,7168]{2,1,0:T(8,128)(2,1)S(1)}, u32[]{:S(2)}, u32[]{:S(2)}) async-start(bf16[8,18,7168]{2,1,0:T(8,128)(2,1)} %reshape.87), calls=%async_computation.2 | async-start | bytes 5505024 | tf_op jit(solution)/shard_map/all_to_all | solution.py:106
  647.8 93.1 %reduce-scatter.4.cloned.1.call-start = ((), (), s32[]{:S(2)}) async-start(), calls=%async_computation.4 | async-start | bytes 1146880
  712.6 3.1 copy-start.1
  715.8 3.0 copy-start.5
Sparse Core Ops, SparseCore 0:
  715.9 24.9 reduce-scatter.3
where the time goes:
time: 749 us; the launch traced here: 748 us
  waiting for transfers between devices  614 us (82%)
  blocking collectives  42.5 us (6%)
  matrix products  26.1 us (3%)
  local copies, waits for them, and re-layouts  24.1 us (3%)
  starting transfers between devices  24 us (3%)
  between operations  14.9 us (2%)
    all_to_all x1, waiting for transfers between devices, shards(): lax.all_to_all(send_cot.reshape(expert_count, cap_col, width), 'expert',...  285 us
    ppermute x3, waiting for transfers between devices, from_partner(): lax.ppermute(x, axis, [(i, i ^ 1 << distance) for i in range(lax.axis_siz...  150 us
    all_to_all x1, waiting for transfers between devices, shards(): lax.all_to_all(send_in.reshape(expert_count, cap_col, width), 'expert', s...  101 us
    all_to_all x1, waiting for transfers between devices, shards(): lax.all_to_all(parts, 'expert', split_axis=0, concat_axis=0, tiled=True)  63 us
    unnamed x2, waiting for transfers between devices  16 us
  transfers between devices with their start and end apart: 7, of which 6 were waited for; matrix products, arithmetic and copies ran while one was open for 5% of the time, Pallas kernels for 0%

commit v1 on v0

--- a/solution.py
+++ b/solution.py
@@ -119,6 +119,77 @@
     )
 
 
+def dense_shards(tokens, cotangent, w_gate, w_up, w_down, routes, gates, matching):
+    axes = ("expert", "dp")
+    rows_here, width = tokens.shape[2:]
+    topk = routes.shape[3]
+    units = w_gate.shape[2]
+    expert_count = lax.axis_size("expert")
+    group_count = lax.axis_size("dp")
+    cap_col = 3 * group_count * rows_here * topk // (2 * expert_count)
+    slot_count = expert_count * cap_col
+    self_index = lax.axis_index("expert")
+    pair_bit = expert_count.bit_length() - 2
+    expert_iota = jnp.arange(expert_count, dtype=jnp.int32)
+    partner = jnp.sum(jnp.where(expert_iota == self_index, matching, 0))
+    flipped = partner != self_index
+    labels = jnp.concatenate([routes[0, 0], gates[0, 0]], axis=1)
+    labels = lax.all_gather(labels, axes, axis=0, tiled=True)
+    rows = lax.all_gather(tokens[0, 0], axes, axis=0, tiled=True)
+    cots = lax.all_gather(cotangent[0, 0], axes, axis=0, tiled=True)
+    route, gate = labels[:, :topk], labels[:, topk:]
+    count = route.shape[0]
+
+    def picks(expert):
+        hit = jnp.any(route == expert, axis=1)
+        at = jnp.arange(count, dtype=jnp.int32)
+        ranking = jnp.sum((at[None, :] < at[:, None]) & hit[None, :], axis=1, dtype=jnp.int32)
+        slots = jnp.arange(slot_count, dtype=jnp.int32)
+        return ((ranking[None, :] == slots[:, None]) & hit[None, :]).astype(jnp.bfloat16)
+
+    weight = jnp.sum(jnp.where(route == self_index, gate, 0), axis=1).astype(jnp.float32) / 65536.0
+    weight = weight[:, None]
+    gate_act = jnp.dot(rows, w_gate[0], preferred_element_type=jnp.float32)
+    up_act = jnp.dot(rows, w_up[0], preferred_element_type=jnp.float32)
+    d_hidden = contract_units(cots, w_down[0]) * weight
+    sigmoid_gate = jax.nn.sigmoid(gate_act)
+    hidden = (gate_act * sigmoid_gate * up_act * weight).astype(jnp.bfloat16)
+    d_gate = (d_hidden * up_act * sigmoid_gate * (1.0 + gate_act * (1.0 - sigmoid_gate))).astype(
+        jnp.bfloat16
+    )
+    d_up = (d_hidden * gate_act * sigmoid_gate).astype(jnp.bfloat16)
+    factors = jnp.concatenate([d_gate, d_up, hidden], axis=1)
+    packed = jnp.dot(picks(self_index), factors, preferred_element_type=jnp.float32)
+    packed = packed.astype(jnp.bfloat16)
+    swapped = from_partner(packed, "expert", pair_bit)
+    partial = contract_units(d_gate, w_gate[0]) + contract_units(d_up, w_up[0])
+    total = lax.psum_scatter(
+        partial.astype(jnp.bfloat16).reshape(-1, rows_here, width),
+        axes,
+        scatter_dimension=0,
+        tiled=True,
+    )
+    chosen = jnp.where(flipped, swapped, packed)
+    spread = contract_rows(picks(partner), chosen).astype(jnp.bfloat16)
+    grad_gate = contract_rows(rows, spread[:, :units]).astype(jnp.bfloat16)
+    grad_up = contract_rows(rows, spread[:, units : 2 * units]).astype(jnp.bfloat16)
+    grad_down = contract_rows(spread[:, 2 * units :], cots).astype(jnp.bfloat16)
+    return (
+        total.reshape(1, 1, rows_here, width),
+        grad_gate[None],
+        grad_up[None],
+        grad_down[None],
+    )
+
+
+DENSE_ROWS = 1024
+
+
+def step(tokens, *rest):
+    rows = lax.axis_size("expert") * lax.axis_size("dp") * tokens.shape[2]
+    return (dense_shards if rows <= DENSE_ROWS else shards)(tokens, *rest)
+
+
 def solution(mesh):
     placed = (
         P("expert", "dp", None, None),
@@ -131,7 +202,7 @@
         P(),
     )
     return jax.shard_map(
-        shards,
+        step,
         mesh=mesh,
         in_specs=placed,
         out_specs=(

time: 749 us -> 386 us (0.52)
  waiting for transfers between devices: 614 us -> 221 us
  blocking collectives: 42.5 us -> 71.6 us
  starting transfers between devices: 24 us -> 1.93 us
  matrix products: 26.1 us -> 39.9 us
  local copies, waits for them, and re-layouts: 24.1 us -> 33.4 us
    all_to_all x3 -> x0, waiting for transfers between devices: 449 us -> none  [the longest x1 285 us: shards(): lax.all_to_all(send_cot.reshape(expert_count, cap_col, width), 'expert',...]
    ppermute x3 -> x1, waiting for transfers between devices: 150 us -> 12.5 us  [from_partner(): lax.ppermute(x, axis, [(i, i ^ 1 << distance) for i in range(lax.axis_siz...]
    reduce_scatter x0 -> x1, waiting for transfers between devices: none -> 109 us  [dense_shards(): lax.psum_scatter(partial.astype(jnp.bfloat16).reshape(-1, rows_here, widt...]
    all_gather x0 -> x2, waiting for transfers between devices: none -> 100 us  [the longest x1 80.3 us: dense_shards(): cots = lax.all_gather(cotangent[0, 0], axes, axis=0, tiled=True)]
    all_gather x4 -> x1, blocking collectives: 42.5 us -> 71.6 us  [dense_shards(): labels = lax.all_gather(labels, axes, axis=0, tiled=True)]
    unnamed x20 -> x18, local copies, waits for them, and re-layouts: 0.05 us -> 25.4 us
    all_to_all x3 -> x0, starting transfers between devices: 18.1 us -> none  [the longest x1 8.61 us: shards(): lax.all_to_all(parts, 'expert', split_axis=0, concat_axis=0, tiled=True)]
    unnamed x2 -> x3, waiting for transfers between devices: 16 us -> 0.05 us
  transfers between devices with their start and end apart: 7 -> 4, of which waited for: 6 -> 4; matrix products, arithmetic and copies ran while one was open for 5% -> 12% of each run, Pallas kernels for 0% -> 0%
where the time goes in v1:
time: 386 us; the launch traced here: 385 us
  waiting for transfers between devices  221 us (57%)
  blocking collectives  71.6 us (19%)
  matrix products  39.9 us (10%)
  local copies, waits for them, and re-layouts  33.4 us (9%)
  between operations  14.5 us (4%)
    reduce_scatter x1, waiting for transfers between devices, dense_shards(): lax.psum_scatter(partial.astype(jnp.bfloat16).reshape(-1, rows_here, widt...  109 us
    all_gather x1, waiting for transfers between devices, dense_shards(): cots = lax.all_gather(cotangent[0, 0], axes, axis=0, tiled=True)  80.3 us
    all_gather x1, blocking collectives, dense_shards(): labels = lax.all_gather(labels, axes, axis=0, tiled=True)  71.6 us
    unnamed x18, local copies, waits for them, and re-layouts  25.4 us
    dot_general x4, matrix products, contract_rows(): lax.dot_general(left, right, (((0,), (0,)), ((), ())), preferred_element_...  22 us
    all_gather x1, waiting for transfers between devices, dense_shards(): rows = lax.all_gather(tokens[0, 0], axes, axis=0, tiled=True)  19.8 us
    dot_general x3, matrix products, contract_units(): lax.dot_general(left, right, (((1,), (1,)), ((), ())), preferred_element_...  13.3 us
    ppermute x1, waiting for transfers between devices, from_partner(): lax.ppermute(x, axis, [(i, i ^ 1 << distance) for i in range(lax.axis_siz...  12.5 us
  transfers between devices with their start and end apart: 4, of which 4 were waited for; matrix products, arithmetic and copies ran while one was open for 12% of the time, Pallas kernels for 0%

profile of v1, /device:TPU:0, one launch (start us, length us, event | category | flops | bytes accessed | tf_op | source)
XLA Modules:
  0.0 385.1 jit_solution(6186300054382726149)
XLA Ops:
  7.2 1.9 copy.29
  9.2 0.0 all-gather.6.cloned.1.call-start
  9.2 1.9 copy.27
  11.2 0.7 add_bitcast_fusion
  11.9 71.6 %all-gather.2 = s32[32,12,4]{1,2,0:T(4,128)S(1)} all-gather(s32[1,12,4]{1,2,0:T(4,128)S(1)} %add_bitcast_fusion), channel_id=1, replica_groups=mesh['dp'=4,'expert'=8] {'expert','dp'}, dimensions={0}, use_global_device_ids=true | all-gather | bytes 6336 | tf_op jit(solution)/shard_map/all_gather | solution.py:137
  83.5 0.1 reshape.27
  83.7 19.8 %all-gather.8.cloned.1.call-done = bf16[1,1,384,7168]{3,1,0,2:T(2,128)(2,1)} async-done(((bf16[1,1,12,7168]{3,1,0,2:T(2,128)(2,1)}), bf16[1,1,384,7168]{3,1,0,2:T(2,128)(2,1)}) %all-gather.8.cloned.1.call-update) | async-done | bytes 5505040 | tf_op jit(solution)/shard_map/all_gather | solution.py:138
  103.5 6.1 %copy.33 = bf16[1,1,384,7168]{3,2,0,1:T(8,128)(2,1)S(1)} copy(bf16[1,1,384,7168]{3,1,0,2:T(2,128)(2,1)} %all-gather.8.cloned.1.call-done) | data formatting | bytes 11010048
  109.6 2.4 copy-done
  112.1 2.1 fusion.5
  114.2 80.3 %all-gather.6.cloned.1.call-done = bf16[1,1,384,7168]{3,1,0,2:T(2,128)(2,1)} async-done(((bf16[1,1,12,7168]{3,1,0,2:T(2,128)(2,1)}), bf16[1,1,384,7168]{3,1,0,2:T(2,128)(2,1)}) %all-gather.6.cloned.1.call-update) | async-done | bytes 5505040 | tf_op jit(solution)/shard_map/all_gather | solution.py:139
  194.5 7.4 %fusion.20 = f32[384,256]{0,1:T(8,128)S(1)} fusion(bf16[1,256,7168]{2,1,0:T(8,128)(2,1)} %param.12, bf16[1,1,384,7168]{3,1,0,2:T(2,128)(2,1)} %all-gather.6.cloned.1.call-done, f32[384]{0:T(512)S(1)} %convert_multiply_fusion), kind=kOutput, calls=%fused_computation.25 | convolution fusion | flops 1409384448 | bytes 9569792 | tf_op jit(solution)/shard_map/dot_general | solution.py:28
  201.9 0.4 copy-done.4
  202.3 2.2 multiply_convert_fusion
  204.6 1.7 fusion.12
  206.3 4.1 %add_convert_fusion = bf16[384,7168]{1,0:T(8,128)(2,1)} fusion(f32[384,7168]{1,0:T(8,128)S(1)} %fusion.12, bf16[384,256]{0,1:T(8,128)(2,1)S(1)} %get-tuple-element.28, bf16[1,7168,256]{2,1,0:T(8,128)(2,1)S(1)} %copy-done.4), kind=kOutput, calls=%fused_computation | convolution fusion | flops 1414791168 | bytes 20381696 | tf_op jit(solution)/shard_map/dot_general | solution.py:28
  210.4 8.0 %reshape.22 = bf16[32,12,7168]{2,1,0:T(8,128)(2,1)} reshape(bf16[384,7168]{1,0:T(8,128)(2,1)} %add_convert_fusion) | data formatting | bytes 11010048 | tf_op jit(solution)/shard_map/reshape | solution.py:167
  218.4 0.6 copy-done.5
  219.1 0.6 fusion.46
  219.7 0.7 compare_reduce_fusion
  220.4 0.1 convert_reduce_fusion
  220.5 0.3 convolution_convert_fusion.4
  220.8 1.8 collective-permute-start
  223.3 0.1 convert_reduce_fusion.1
  223.4 12.5 %collective-permute-done = bf16[144,768]{1,0:T(8,128)(2,1)S(1)} collective-permute-done((bf16[144,768]{1,0:T(8,128)(2,1)S(1)}, bf16[144,768]{1,0:T(8,128)(2,1)S(1)}, u32[]{:S(2)}, u32[]{:S(2)}) %collective-permute-start) | collective-permute-done | bytes 221216 | tf_op jit(solution)/shard_map/ppermute | solution.py:8
  235.9 0.4 convolution_convert_fusion.3
  236.3 6.5 %fusion = bf16[1,7168,256]{1,2,0:T(8,128)(2,1)} fusion(bf16[1,1,384,7168]{3,2,0,1:T(8,128)(2,1)} %copy-done, bf16[384,768]{1,0:T(8,128)(2,1)S(1)} %convolution_convert_fusion.3), kind=kOutput, calls=%fused_computation.4 | convolution fusion | flops 1411121152 | bytes 9371648 | tf_op jit(solution)/shard_map/dot_general | solution.py:22
  242.8 5.9 %copy.30 = bf16[1,7168,256]{2,1,0:T(8,128)(2,1)} copy(bf16[1,7168,256]{1,2,0:T(8,128)(2,1)} %fusion) | data formatting | bytes 7340032
  248.7 6.5 %fusion.1 = bf16[1,7168,256]{1,2,0:T(8,128)(2,1)} fusion(bf16[1,1,384,7168]{3,2,0,1:T(8,128)(2,1)} %copy-done, bf16[384,768]{1,0:T(8,128)(2,1)S(1)} %convolution_convert_fusion.3), kind=kOutput, calls=%fused_computation.5 | convolution fusion | flops 1411121152 | bytes 9371648 | tf_op jit(solution)/shard_map/dot_general | solution.py:22
  255.3 5.9 %copy.31 = bf16[1,7168,256]{2,1,0:T(8,128)(2,1)} copy(bf16[1,7168,256]{1,2,0:T(8,128)(2,1)} %fusion.1) | data formatting | bytes 7340032
  261.2 8.5 %fusion.2 = bf16[1,256,7168]{2,1,0:T(8,128)(2,1)} fusion(bf16[1,1,384,7168]{3,1,0,2:T(2,128)(2,1)} %all-gather.6.cloned.1.call-done, bf16[384,768]{1,0:T(8,128)(2,1)S(1)} %convolution_convert_fusion.3), kind=kOutput, calls=%fused_computation.6 | convolution fusion | flops 1411121152 | bytes 9371648 | tf_op jit(solution)/shard_map/dot_general | solution.py:22
  269.7 108.9 %reduce-scatter.2.cloned.1.call-done = bf16[1,12,7168]{2,1,0:T(8,128)(2,1)} async-done(((bf16[32,12,7168]{2,1,0:T(8,128)(2,1)}), bf16[1,12,7168]{2,1,0:T(8,128)(2,1)}) %reduce-scatter.2.cloned.1.call-update) | async-done | bytes 172048 | tf_op jit(solution)/shard_map/reduce_scatter | solution.py:166
  (17 shorter events, 0.2 us)
Async XLA Ops:
  7.2 96.3 %all-gather.8.cloned.1.call-start = ((), (), s32[]{:S(2)}) async-start(), calls=%async_computation.3 | async-start | bytes 11354112 | tf_op jit(solution)/shard_map/all_gather | solution.py:138
  9.2 185.3 %all-gather.6.cloned.1.call-start = ((), (), s32[]{:S(2)}) async-start(), calls=%async_computation.2 | async-start | bytes 11354112 | tf_op jit(solution)/shard_map/all_gather | solution.py:139
  11.2 367.4 %reduce-scatter.2.cloned.1.call-start = ((), (), s32[]{:S(2)}) async-start(), calls=%async_computation.1 | async-start | bytes 7569408 | tf_op jit(solution)/shard_map/reduce_scatter | solution.py:166
  103.5 8.6 %copy-start.2 = (bf16[1,7168,256]{2,1,0:T(8,128)(2,1)S(1)}, bf16[1,7168,256]{2,1,0:T(8,128)(2,1)}, u32[]{:S(2)}) copy-start(bf16[1,7168,256]{2,1,0:T(8,128)(2,1)} %param.10) | copy-start | bytes 11010052
  109.6 2.4 copy-start
  194.5 7.5 %copy-start.1 = (bf16[1,1,384,7168]{3,2,0,1:T(8,128)(2,1)S(1)}, bf16[1,1,384,7168]{3,2,0,1:T(8,128)(2,1)}, u32[]{:S(2)}) copy-start(bf16[1,1,384,7168]{3,2,0,1:T(8,128)(2,1)} %copy-done) | copy-start | bytes 16515076
  194.5 7.8 %copy-start.4 = (bf16[1,7168,256]{2,1,0:T(8,128)(2,1)S(1)}, bf16[1,7168,256]{2,1,0:T(8,128)(2,1)}, u32[]{:S(2)}) copy-start(bf16[1,7168,256]{2,1,0:T(8,128)(2,1)} %param.11) | copy-start | bytes 11010052
  202.3 2.2 copy-start.3
  218.4 0.7 copy-start.5
  220.8 15.1 %collective-permute-start = (bf16[144,768]{1,0:T(8,128)(2,1)S(1)}, bf16[144,768]{1,0:T(8,128)(2,1)S(1)}, u32[]{:S(2)}, u32[]{:S(2)}) collective-permute-start(bf16[144,768]{1,0:T(8,128)(2,1)S(1)} %convolution_convert_fusion.4), channel_id=1, source_target_pairs={{0,4},{1,5},{2,6},{3,7},{4,0},{5,1},{6,2},{7,3},{8,12},{9,13},{10,... | collective-permute-start | bytes 663560 | tf_op jit(solution)/shard_map/ppermute | solution.py:8
Sparse Core Ops, SparseCore 0:
  11.5 91.9 all-gather.7
  107.0 87.4 all-gather.5
  218.5 159.9 reduce-scatter.1

commit v2 on v0

--- a/solution.py
+++ b/solution.py
@@ -1,7 +1,15 @@
 import jax
 import jax.numpy as jnp
+import numpy as np
 from jax import lax
+from jax.experimental import pallas as pl
+from jax.experimental.pallas import tpu as pltpu
 from jax.sharding import PartitionSpec as P
+
+MESH = pl.DeviceIdType.MESH
+LANES = 128
+ROW_TILE = 8
+CHUNKS = 2
 
 
 def from_partner(x, axis, distance):
@@ -119,6 +127,320 @@
     )
 
 
+def flip(index, bit):
+    return index + bit - 2 * bit * lax.rem(lax.div(index, bit), 2)
+
+
+def greet(peers):
+    barrier = pltpu.get_barrier_semaphore()
+    for peer in peers:
+        place = {"expert": peer[0], "dp": peer[1]}
+        pl.semaphore_signal(barrier, inc=1, device_id=place, device_id_type=MESH)
+    pl.semaphore_wait(barrier, len(peers))
+
+
+def remote(src, dst, sems, index, peer):
+    return pltpu.make_async_remote_copy(
+        src_ref=src,
+        dst_ref=dst,
+        send_sem=sems[0].at[index],
+        recv_sem=sems[1].at[index],
+        device_id={"expert": peer[0], "dp": peer[1]},
+        device_id_type=MESH,
+    )
+
+
+def gather_kernel(own_ref, out_ref, local_sem, send_sem, recv_sem):
+    me, group = lax.axis_index("expert"), lax.axis_index("dp")
+    sems = (send_sem, recv_sem)
+    along_x, along_y = (me, flip(group, 1)), (me, flip(group, 2))
+    near, far, sibling = (flip(me, 2), group), (flip(me, 4), group), (flip(me, 1), group)
+    level = [me, flip(me, 2), flip(me, 4), flip(flip(me, 4), 2)]
+    spot = [group, flip(group, 1), flip(group, 2), flip(flip(group, 2), 1)]
+    z_at, x_at, y_at, diag_at, sib_at = 0, 4, 8, 12, 20
+    copies = {}
+
+    def slab(z, d):
+        return out_ref.at[:, level[z], spot[d]]
+
+    def send(index, src, dst, peer):
+        copies[index] = remote(src, dst, sems, index, peer)
+        copies[index].start()
+
+    def arrived(index):
+        copies[index].wait_recv()
+
+    greet([along_x, along_y, near, far, sibling])
+    keep = pltpu.make_async_copy(own_ref, slab(0, 0), local_sem)
+    keep.start()
+
+    def spread(z):
+        src = own_ref if z == 0 else slab(z, 0)
+        send(x_at + z, src, slab(z, 0), along_x)
+        send(y_at + z, src, slab(z, 0), along_y)
+        send(sib_at + 4 * z, src, slab(z, 0), sibling)
+
+    def corners(z):
+        for d, at, half, peer in ((1, x_at, 0, along_y), (2, y_at, 1, along_x)):
+            arrived(at + z)
+            part = out_ref.at[half, level[z], spot[d]]
+            send(diag_at + 2 * z + half, part, part, peer)
+            send(sib_at + 4 * z + d, slab(z, d), slab(z, d), sibling)
+
+    def finish(z):
+        for half in range(2):
+            arrived(diag_at + 2 * z + half)
+        send(sib_at + 4 * z + 3, slab(z, 3), slab(z, 3), sibling)
+
+    send(z_at + 2, own_ref, slab(0, 0), far)
+    send(z_at + 1, own_ref, slab(0, 0), near)
+    spread(0)
+    corners(0)
+    arrived(z_at + 1)
+    spread(1)
+    arrived(z_at + 2)
+    send(z_at + 3, slab(2, 0), slab(2, 0), near)
+    spread(2)
+    finish(0)
+    corners(1)
+    arrived(z_at + 3)
+    spread(3)
+    corners(2)
+    finish(1)
+    corners(3)
+    finish(2)
+    finish(3)
+    for z in range(4):
+        for d in range(4):
+            arrived(sib_at + 4 * z + d)
+    for copy in copies.values():
+        copy.wait_send()
+    keep.wait()
+
+
+def gather_all(own):
+    halves, rows, columns = own.shape
+    experts, groups = lax.axis_size("expert"), lax.axis_size("dp")
+    return pl.pallas_call(
+        gather_kernel,
+        out_shape=jax.ShapeDtypeStruct((halves, experts, groups, rows, columns), own.dtype),
+        in_specs=[pl.BlockSpec(memory_space=pl.ANY)],
+        out_specs=pl.BlockSpec(memory_space=pl.ANY),
+        scratch_shapes=[
+            pltpu.SemaphoreType.DMA,
+            pltpu.SemaphoreType.DMA((36,)),
+            pltpu.SemaphoreType.DMA((36,)),
+        ],
+        compiler_params=pltpu.CompilerParams(collective_id=0, has_side_effects=True),
+    )(own)
+
+
+def return_kernel(
+    parts_ref, packed_ref, widen_ref, place_ref, out_ref, swapped_ref,
+    first, second, second_in, third, third_in, send_sem, recv_sem,
+):
+    me, group = lax.axis_index("expert"), lax.axis_index("dp")
+    experts = second.shape[1]
+    sems = (send_sem, recv_sem)
+    mates = [group, flip(group, 1), flip(group, 2), flip(flip(group, 2), 1)]
+    others = [lax.rem(me + m, experts) for m in range(experts)]
+    step = 6 + experts
+    copies = {}
+
+    def send(index, src, dst, peer):
+        copies[index] = remote(src, dst, sems, index, peer)
+        copies[index].start()
+
+    greet([(me, mates[r]) for r in (1, 2, 3)] + [(others[m], group) for m in range(1, experts)])
+    send(CHUNKS * step, packed_ref, swapped_ref, (flip(me, experts // 2), group))
+    for c in range(CHUNKS):
+        for r in (3, 1, 2):
+            send(c * step + r, parts_ref.at[mates[r] * CHUNKS + c], first.at[c, r], (me, mates[r]))
+    for c in range(CHUNKS):
+        total = parts_ref[group * CHUNKS + c].astype(jnp.float32)
+        for r in (1, 2, 3):
+            copies[c * step + r].wait_recv()
+            total = total + first[c, r].astype(jnp.float32)
+        total = total.astype(jnp.bfloat16)
+        for i in range(experts):
+            block = jnp.dot(widen_ref[i], total, preferred_element_type=jnp.float32)
+            second[c, i] = block.astype(jnp.bfloat16)
+        for m in (4, 5, 3, 6, 2, 7, 1):
+            send(c * step + 3 + m, second.at[c, others[m]], second_in.at[c, me], (others[m], group))
+        second_in[c, me] = second[c, me]
+    for c in range(CHUNKS):
+        for m in range(1, experts):
+            copies[c * step + 3 + m].wait_recv()
+        total = jnp.zeros((place_ref.shape[1], second.shape[3]), jnp.float32)
+        for i in range(experts):
+            total = total + jnp.dot(
+                place_ref[i], second_in[c, i], preferred_element_type=jnp.float32
+            )
+        total = total.astype(jnp.bfloat16)
+        rows = third.shape[2]
+        for r in range(4):
+            third[c, r] = total[r * rows : (r + 1) * rows]
+        for r in (3, 1, 2):
+            send(c * step + 2 + experts + r, third.at[c, mates[r]], third_in.at[c, group], (me, mates[r]))
+        third_in[c, group] = third[c, group]
+    for c in range(CHUNKS):
+        for r in (1, 2, 3):
+            copies[c * step + 2 + experts + r].wait_recv()
+        columns = third.shape[3]
+        for r in range(4):
+            at = (r * CHUNKS + c) * columns
+            out_ref[:, at : at + columns] = third_in[c, r]
+    copies[CHUNKS * step].wait_recv()
+    for copy in copies.values():
+        copy.wait_send()
+
+
+def return_all(parts, packed, widen, place, rows_out):
+    pieces, slots, columns = parts.shape
+    experts, wide = widen.shape[:2]
+    groups = pieces // CHUNKS
+    vmem = pl.BlockSpec(memory_space=pltpu.VMEM)
+    count = CHUNKS * (6 + experts) + 1
+    return pl.pallas_call(
+        return_kernel,
+        out_shape=(
+            jax.ShapeDtypeStruct((rows_out, pieces * columns), jnp.bfloat16),
+            jax.ShapeDtypeStruct(packed.shape, packed.dtype),
+        ),
+        in_specs=[vmem] * 4,
+        out_specs=(vmem, vmem),
+        scratch_shapes=[
+            pltpu.VMEM((CHUNKS, 4, slots, columns), jnp.bfloat16),
+            pltpu.VMEM((CHUNKS, experts, wide, columns), jnp.bfloat16),
+            pltpu.VMEM((CHUNKS, experts, wide, columns), jnp.bfloat16),
+            pltpu.VMEM((CHUNKS, groups, rows_out, columns), jnp.bfloat16),
+            pltpu.VMEM((CHUNKS, groups, rows_out, columns), jnp.bfloat16),
+            pltpu.SemaphoreType.DMA((count,)),
+            pltpu.SemaphoreType.DMA((count,)),
+        ],
+        compiler_params=pltpu.CompilerParams(
+            collective_id=1, has_side_effects=True, vmem_limit_bytes=48 * 2**20
+        ),
+    )(parts, packed, widen, place)
+
+
+def small_shards(tokens, cotangent, w_gate, w_up, w_down, routes, gates, matching):
+    rows_here, width = tokens.shape[2:]
+    topk = routes.shape[3]
+    units = w_gate.shape[2]
+    half = width // 2
+    expert_count = lax.axis_size("expert")
+    group_count = lax.axis_size("dp")
+    column_tok = group_count * rows_here
+    cap_col = 3 * group_count * rows_here * topk // (2 * expert_count)
+    slot_count = expert_count * cap_col
+    self_index = lax.axis_index("expert")
+    expert_iota = jnp.arange(expert_count, dtype=jnp.int32)
+    partner = jnp.sum(jnp.where(expert_iota == self_index, matching, 0))
+    flipped = partner != self_index
+    gate_here = gates[0, 0]
+    labels = jnp.concatenate([routes[0, 0], gate_here // 256, gate_here % 256], axis=1)
+    labels = jnp.pad(labels, ((0, rows_here), (0, LANES - 3 * topk))).astype(jnp.bfloat16)
+    body = jnp.concatenate([tokens[0, 0], cotangent[0, 0]], axis=0)
+    own = jnp.stack(
+        [
+            jnp.concatenate([body[:, :half], labels], axis=1),
+            jnp.concatenate([body[:, half:], labels], axis=1),
+        ]
+    )
+    everything = gather_all(own)
+    labels = everything[0, :, :, :rows_here, half : half + 3 * topk].astype(jnp.int32)
+    labels = labels.reshape(expert_count, column_tok, 3, topk)
+    route = labels[:, :, 0]
+    gate = labels[:, :, 1] * 256 + labels[:, :, 2]
+    rows_all = everything.reshape(2, expert_count * group_count * 2 * rows_here, half + LANES)
+
+    def ranked(expert):
+        hit = jnp.any(route == expert, axis=2)
+        at = jnp.arange(column_tok, dtype=jnp.int32)
+        before = (at[None, :] < at[:, None])[None] & hit[:, None, :]
+        ranking = jnp.sum(before, axis=2, dtype=jnp.int32)
+        slot = expert_iota[:, None] * cap_col + ranking
+        return jnp.where(hit, slot, -1).reshape(expert_count, group_count, rows_here)
+
+    def picked(expert):
+        slot = ranked(expert)
+        none = jnp.full_like(slot, -1)
+        from_tok = jnp.concatenate([slot, none], axis=2).reshape(-1)
+        from_cot = jnp.concatenate([none, slot], axis=2).reshape(-1)
+        iota = jnp.arange(slot_count, dtype=jnp.int32)[:, None]
+        pick = jnp.concatenate([from_tok[None] == iota, from_cot[None] == iota], axis=0)
+        pick = pick.astype(jnp.bfloat16)
+        return [
+            jnp.dot(pick, rows_all[i], preferred_element_type=jnp.float32)[:, :half].astype(
+                jnp.bfloat16
+            )
+            for i in range(2)
+        ]
+
+    weight = jnp.sum(jnp.where(route == self_index, gate, 0), axis=2).reshape(-1)
+    own_slot = ranked(self_index).reshape(-1)
+    slot_iota = jnp.arange(slot_count, dtype=jnp.int32)[:, None]
+    weight = jnp.sum(jnp.where(own_slot[None] == slot_iota, weight[None], 0), axis=1)
+    weight = (weight.astype(jnp.float32) / 65536.0)[:, None]
+    mine = picked(self_index)
+    rows_in = jnp.concatenate([block[:slot_count] for block in mine], axis=1)
+    rows_cot = jnp.concatenate([block[slot_count:] for block in mine], axis=1)
+    rows_cot = (rows_cot.astype(jnp.float32) * weight).astype(jnp.bfloat16)
+    gate_act = jnp.dot(rows_in, w_gate[0], preferred_element_type=jnp.float32)
+    up_act = jnp.dot(rows_in, w_up[0], preferred_element_type=jnp.float32)
+    d_hidden = contract_units(rows_cot, w_down[0])
+    sigmoid_gate = jax.nn.sigmoid(gate_act)
+    hidden = (gate_act * sigmoid_gate * up_act * weight).astype(jnp.bfloat16)
+    d_gate = (d_hidden * up_act * sigmoid_gate * (1.0 + gate_act * (1.0 - sigmoid_gate))).astype(
+        jnp.bfloat16
+    )
+    d_up = (d_hidden * gate_act * sigmoid_gate).astype(jnp.bfloat16)
+    packed = jnp.concatenate([d_gate, d_up, hidden], axis=1)
+    pieces = group_count * CHUNKS
+    partial = contract_units(d_gate, w_gate[0]) + contract_units(d_up, w_up[0])
+    parts = partial.astype(jnp.bfloat16).reshape(slot_count, pieces, width // pieces)
+    parts = parts.transpose(1, 0, 2)
+    wide = -(-cap_col // ROW_TILE) * ROW_TILE
+    widen = np.zeros((expert_count, wide, slot_count), np.float32)
+    for i in range(expert_count):
+        widen[i, np.arange(cap_col), i * cap_col + np.arange(cap_col)] = 1.0
+    column_route = jnp.sum(
+        jnp.where(expert_iota[:, None, None] == self_index, route, 0), axis=0
+    )
+    hits = jnp.any(column_route[None] == expert_iota[:, None, None], axis=2)
+    at = jnp.arange(column_tok, dtype=jnp.int32)
+    ranking = jnp.sum(
+        (at[None, :] < at[:, None])[None] & hits[:, None, :], axis=2, dtype=jnp.int32
+    )
+    place = (ranking[:, :, None] == jnp.arange(wide)[None, None]) & hits[:, :, None]
+    rows_out = -(-rows_here // 16) * 16
+    place = place.reshape(expert_count, group_count, rows_here, wide)
+    place = jnp.pad(place, ((0, 0), (0, 0), (0, rows_out - rows_here), (0, 0)))
+    place = place.reshape(expert_count, group_count * rows_out, wide).astype(jnp.bfloat16)
+    total, swapped = return_all(
+        parts, packed, jnp.asarray(widen, jnp.bfloat16), place, rows_out
+    )
+    chosen = jnp.where(flipped, swapped, packed)
+    theirs = picked(partner)
+    their_rows = jnp.concatenate([block[:slot_count] for block in theirs], axis=1)
+    their_cot = jnp.concatenate([block[slot_count:] for block in theirs], axis=1)
+    grad_gate = contract_rows(their_rows, chosen[:, :units]).astype(jnp.bfloat16)
+    grad_up = contract_rows(their_rows, chosen[:, units : 2 * units]).astype(jnp.bfloat16)
+    grad_down = contract_rows(chosen[:, 2 * units :], their_cot).astype(jnp.bfloat16)
+    return (
+        total[:rows_here].reshape(1, 1, rows_here, width),
+        grad_gate[None],
+        grad_up[None],
+        grad_down[None],
+    )
+
+
+def step(tokens, *rest):
+    small = lax.axis_size("expert") == 8 and lax.axis_size("dp") == 4
+    return (small_shards if small else shards)(tokens, *rest)
+
+
 def solution(mesh):
     placed = (
         P("expert", "dp", None, None),
@@ -131,7 +453,7 @@
         P(),
     )
     return jax.shard_map(
-        shards,
+        step,
         mesh=mesh,
         in_specs=placed,
         out_specs=(

time: 749 us -> 152 us (0.20)
  waiting for transfers between devices: 614 us -> 0 us
  Pallas kernels: 0 us -> 99.2 us
  blocking collectives: 42.5 us -> 0 us
  starting transfers between devices: 24 us -> 0 us
  between operations: 14.9 us -> 1.65 us
    all_to_all x3 -> x0, waiting for transfers between devices: 449 us -> none  [the longest x1 285 us: shards(): lax.all_to_all(send_cot.reshape(expert_count, cap_col, width), 'expert',...]
    ppermute x3 -> x0, waiting for transfers between devices: 150 us -> none  [from_partner(): lax.ppermute(x, axis, [(i, i ^ 1 << distance) for i in range(lax.axis_siz...]
    pallas_call x0 -> x2, Pallas kernels: none -> 99.2 us  [the longest x1 56.1 us: gather_all(): pl.pallas_call(gather_kernel, out_shape=jax.ShapeDtypeStruct((halves, exp...]
    all_gather x4 -> x0, blocking collectives: 42.5 us -> none  [the longest x1 12.7 us: shards(): lax.all_gather(tokens, 'dp', axis=1, tiled=True)]
    all_to_all x3 -> x0, starting transfers between devices: 18.1 us -> none  [the longest x1 8.61 us: shards(): lax.all_to_all(parts, 'expert', split_axis=0, concat_axis=0, tiled=True)]
    unnamed x2 -> x0, waiting for transfers between devices: 16 us -> none
    reshape x7 -> x2, local copies, waits for them, and re-layouts: 12.6 us -> 0.87 us  [the longest x1 0.7 us: small_shards(): total[:rows_here].reshape(1, 1, rows_here, width)]
    slice x0 -> x5, local copies, waits for them, and re-layouts: none -> 10.2 us  [the longest x1 9.65 us: picked(): rows_all[i]]
  transfers between devices with their start and end apart: 7 -> 0, of which waited for: 6 -> 0; matrix products, arithmetic and copies ran while one was open for 5% -> 0% of each run, Pallas kernels for 0% -> 0%
where the time goes in v2:
time: 152 us
  Pallas kernels  99.2 us (65%)
  matrix products  25.3 us (17%)
  local copies, waits for them, and re-layouts  17.5 us (12%)
  other arithmetic  7.93 us (5%)
  between operations  1.65 us (1%)
    pallas_call x1, Pallas kernels, gather_all(): pl.pallas_call(gather_kernel, out_shape=jax.ShapeDtypeStruct((halves, exp...  56.1 us
    pallas_call x1, Pallas kernels, return_all(): pl.pallas_call(return_kernel, out_shape=(jax.ShapeDtypeStruct((rows_out,...  43.1 us
    dot_general x4, matrix products, picked(): jnp.dot(pick, rows_all[i], preferred_element_type=jnp.float32)[:, :half]  10.5 us
    slice x1, local copies, waits for them, and re-layouts, picked(): rows_all[i]  9.65 us
    dot_general x3, matrix products, contract_rows(): lax.dot_general(left, right, (((0,), (0,)), ((), ())), preferred_element_...  9.1 us
    dot_general x3, matrix products, contract_units(): lax.dot_general(left, right, (((1,), (1,)), ((), ())), preferred_element_...  4.27 us
    unnamed x16, local copies, waits for them, and re-layouts  3.97 us

profile of v2, /device:TPU:0, one launch (start us, length us, event | category | flops | bytes accessed | tf_op | source)
XLA Modules:
  0.0 151.6 jit_solution(14612635633540753621)
XLA Ops:
  0.6 1.3 select_reduce_fusion.2
  2.6 0.7 convert_bitcast_fusion
  3.4 0.8 copy.41
  4.3 1.0 fusion.23
  5.3 1.0 fusion.21
  6.3 0.8 pad_maximum_fusion.6.own_ref
  7.1 56.1 %shard_map.120 = bf16[2,8,4,24,3712]{4,3,2,1,0:T(8,128)(2,1)} custom-call(bf16[2,24,3712]{2,1,0:T(8,128)(2,1)} %pad_maximum_fusion.6.own_ref), custom_call_target="tpu_custom_call" | custom-call | tf_op jit(solution)/shard_map/pallas_call | solution.py:224
  63.2 0.9 slice_convert_fusion
  64.1 0.4 copy.46
  64.6 9.6 %fusion.56 = (bf16[1,8,4,24,3712]{4,3,2,1,0:T(8,128)(2,1)}, bf16[1,8,4,24,3712]{4,3,2,1,0:T(8,128)(2,1)}) fusion(bf16[2,8,4,24,3712]{4,3,2,1,0:T(8,128)(2,1)} %shard_map.120), kind=kLoop, calls=%fused_computation.117 | loop fusion | bytes 22806528 | tf_op jit(solution)/shard_map/slice | solution.py:375
  74.3 0.7 fusion.37
  75.3 0.5 convert_reduce_fusion
  77.0 0.2 fusion.20
  77.5 4.6 %convolution_convert_fusion.3 = bf16[288,3712]{1,0:T(8,128)(2,1)S(1)} fusion(bf16[768,3712]{1,0:T(8,128)(2,1)} %bitcast.72, pred[144,768]{1,0:T(8,128)(4,1)S(1)} %iota_compare_fusion, pred[144,768]{1,0:T(8,128)(4,1)S(1)} %iota_compare_fusion.1), kind=kOutput, calls=%fused_computation.8 | convolution fusion | flops 1643360256 | bytes 8060928 | tf_op jit(solution)/shard_map/dot_general | solution.py:375
  82.2 2.0 %convolution_convert_fusion.5 = bf16[288,3712]{1,0:T(8,128)(2,1)S(1)} fusion(bf16[768,3712]{1,0:T(8,128)(2,1)S(1)} %bitcast.75, pred[144,768]{1,0:T(8,128)(4,1)S(1)} %iota_compare_fusion.2, pred[144,768]{1,0:T(8,128)(4,1)S(1)} %iota_compare_fusion.3), kind=kOutput, calls=%fused_computation.10 | convolution fusion | flops 1643360256 | bytes 8060928 | tf_op jit(solution)/shard_map/dot_general | solution.py:375
  84.5 2.0 %convolution_convert_fusion.6 = bf16[288,3712]{1,0:T(8,128)(2,1)S(1)} fusion(bf16[768,3712]{1,0:T(8,128)(2,1)S(1)} %bitcast.70, pred[144,768]{1,0:T(8,128)(4,1)S(1)} %iota_compare_fusion.2, pred[144,768]{1,0:T(8,128)(4,1)S(1)} %iota_compare_fusion.3), kind=kOutput, calls=%fused_computation.11 | convolution fusion | flops 1643360256 | bytes 8060928 | tf_op jit(solution)/shard_map/dot_general | solution.py:375
  86.5 2.0 %convolution_convert_fusion.4 = bf16[288,3712]{1,0:T(8,128)(2,1)S(1)} fusion(bf16[768,3712]{1,0:T(8,128)(2,1)S(1)} %bitcast.71, pred[144,768]{1,0:T(8,128)(4,1)S(1)} %iota_compare_fusion, pred[144,768]{1,0:T(8,128)(4,1)S(1)} %iota_compare_fusion.1), kind=kOutput, calls=%fused_computation.9 | convolution fusion | flops 1643360256 | bytes 8060928 | tf_op jit(solution)/shard_map/dot_general | solution.py:375
  88.8 1.7 %copy-done.3 = bf16[1,256,7168]{2,1,0:T(8,128)(2,1)S(1)} copy-done((bf16[1,256,7168]{2,1,0:T(8,128)(2,1)S(1)}, bf16[1,256,7168]{2,1,0:T(8,128)(2,1)}, u32[]{:S(2)}) %copy-start.3) | copy-done | bytes 3670040
  90.5 1.4 fusion.11
  91.9 0.6 copy-done.1
  92.6 0.7 fusion.6
  93.3 0.9 copy-done.2
  94.1 0.7 multiply_convert_fusion.2
  94.9 1.4 fusion.4
  96.2 1.5 %fusion.3 = bf16[144,7168]{1,0:T(8,128)(2,1)S(1)} fusion(f32[144,7168]{1,0:T(8,128)S(1)} %fusion.4, bf16[144,256]{1,0:T(8,128)(2,1)S(1)} %get-tuple-element.26, bf16[1,7168,256]{2,1,0:T(8,128)(2,1)S(1)} %copy-done.2), kind=kOutput, calls=%fused_computation.7 | convolution fusion | flops 530546688 | bytes 9936896 | tf_op jit(solution)/shard_map/dot_general | solution.py:36
  97.7 0.2 copy.50
  97.9 0.7 copy-done
  98.6 43.1 %shard_map.121 = (bf16[16,7168]{1,0:T(8,128)(2,1)S(1)}, bf16[144,768]{1,0:T(8,128)(2,1)S(1)}) custom-call(bf16[8,144,896]{2,1,0:T(8,128)(2,1)S(1)} %bitcast.65, bf16[144,768]{1,0:T(8,128)(2,1)S(1)} %pad_maximum_fusion.9.packed_ref, bf16[8,24,144]{2,1,0:T(8,128)(2,1)S(1)} %copy-done, bf16[8,64,24]{2,1,0:T(8,128)(2,1)S(1)} %bitcast.66), custom_call_target="tpu_custom_call" | custom-call | tf_op jit(solution)/shard_map/pallas_call | solution.py:304
  141.8 0.7 slice_bitcast_fusion
  142.5 3.0 %fusion.2 = bf16[1,256,7168]{2,1,0:T(8,128)(2,1)} fusion(bf16[144,3584]{1,0:T(8,128)(2,1)S(1)} %get-tuple-element.18, bf16[144,3584]{1,0:T(8,128)(2,1)S(1)} %get-tuple-element.16, bf16[144,768]{1,0:T(8,128)(2,1)S(1)} %broadcast_select_fusion), kind=kOutput, calls=%fused_computation.6 | convolution fusion | flops 534446080 | bytes 5808128 | tf_op jit(solution)/shard_map/dot_general | solution.py:30
  145.5 3.1 %fusion.1 = bf16[1,7168,256]{2,1,0:T(8,128)(2,1)} fusion(bf16[144,3584]{1,0:T(8,128)(2,1)S(1)} %get-tuple-element.19, bf16[144,3584]{1,0:T(8,128)(2,1)S(1)} %get-tuple-element.17, bf16[144,768]{1,0:T(8,128)(2,1)S(1)} %broadcast_select_fusion), kind=kOutput, calls=%fused_computation.5 | convolution fusion | flops 534446080 | bytes 5808128 | tf_op jit(solution)/shard_map/dot_general | solution.py:30
  148.5 3.1 %fusion = bf16[1,7168,256]{2,1,0:T(8,128)(2,1)} fusion(bf16[144,3584]{1,0:T(8,128)(2,1)S(1)} %get-tuple-element.19, bf16[144,3584]{1,0:T(8,128)(2,1)S(1)} %get-tuple-element.17, bf16[144,768]{1,0:T(8,128)(2,1)S(1)} %broadcast_select_fusion), kind=kOutput, calls=%fused_computation.4 | convolution fusion | flops 534446080 | bytes 5808128 | tf_op jit(solution)/shard_map/dot_general | solution.py:30
  (52 shorter events, 2.8 us)
Async XLA Ops:
  77.4 4.8 %slice-start.2 = ((s8[5701632]{0:T(1024)(128)(4,1)}), s8[4194304]{0:T(1024)(128)(4,1)S(1)}, s32[]{:S(2)}) async-start(s8[5701632]{0:T(1024)(128)(4,1)} %bitcast.73), calls=%async_computation.2 | async-start | bytes 8388608
  77.5 4.7 %slice-start.3 = ((s8[5701632]{0:T(1024)(128)(4,1)}), s8[1507328]{0:T(1024)(128)(4,1)S(1)}, s32[]{:S(2)}) async-start(s8[5701632]{0:T(1024)(128)(4,1)} %bitcast.73), calls=%async_computation.3 | async-start | bytes 3014656
  77.5 7.0 %slice-start = ((s8[5701632]{0:T(1024)(128)(4,1)}), s8[4194304]{0:T(1024)(128)(4,1)S(1)}, s32[]{:S(2)}) async-start(s8[5701632]{0:T(1024)(128)(4,1)} %bitcast.68), calls=%async_computation | async-start | bytes 8388608
  82.2 2.3 %slice-start.1 = ((s8[5701632]{0:T(1024)(128)(4,1)}), s8[1507328]{0:T(1024)(128)(4,1)S(1)}, s32[]{:S(2)}) async-start(s8[5701632]{0:T(1024)(128)(4,1)} %bitcast.68), calls=%async_computation.1 | async-start | bytes 3014656
  88.5 2.0 %copy-start.3 = (bf16[1,256,7168]{2,1,0:T(8,128)(2,1)S(1)}, bf16[1,256,7168]{2,1,0:T(8,128)(2,1)}, u32[]{:S(2)}) copy-start(bf16[1,256,7168]{2,1,0:T(8,128)(2,1)} %param.13) | copy-start | bytes 11010052
  90.5 2.0 %copy-start.1 = (bf16[1,7168,256]{2,1,0:T(8,128)(2,1)S(1)}, bf16[1,7168,256]{2,1,0:T(8,128)(2,1)}, u32[]{:S(2)}) copy-start(bf16[1,7168,256]{2,1,0:T(8,128)(2,1)} %param.11) | copy-start | bytes 11010052
  91.9 2.2 %copy-start.2 = (bf16[1,7168,256]{2,1,0:T(8,128)(2,1)S(1)}, bf16[1,7168,256]{2,1,0:T(8,128)(2,1)}, u32[]{:S(2)}) copy-start(bf16[1,7168,256]{2,1,0:T(8,128)(2,1)} %param.12) | copy-start | bytes 11010052
  97.7 0.9 copy-start

commit v3 on v2

--- a/solution.py
+++ b/solution.py
@@ -9,7 +9,8 @@
 MESH = pl.DeviceIdType.MESH
 LANES = 128
 ROW_TILE = 8
-CHUNKS = 2
+CHUNKS = 7
+LAG = 2
 
 
 def from_partner(x, axis, distance):
@@ -150,7 +151,9 @@
     )
 
 
-def gather_kernel(own_ref, out_ref, local_sem, send_sem, recv_sem):
+def gather_kernel(
+    tok_ref, cot_ref, route_ref, gate_ref, out_ref, own_ref, local_sem, send_sem, recv_sem
+):
     me, group = lax.axis_index("expert"), lax.axis_index("dp")
     sems = (send_sem, recv_sem)
     along_x, along_y = (me, flip(group, 1)), (me, flip(group, 2))
@@ -159,9 +162,25 @@
     spot = [group, flip(group, 1), flip(group, 2), flip(flip(group, 2), 1)]
     z_at, x_at, y_at, diag_at, sib_at = 0, 4, 8, 12, 20
     copies = {}
+    rows, width = tok_ref.shape
+    columns = out_ref.shape[3]
+    middle = width // 2
+    topk = route_ref.shape[1]
+    lane = lax.broadcasted_iota(jnp.int32, (rows, columns - width), 1)
+    labels = jnp.zeros_like(lane)
+    for k in range(topk):
+        gate = gate_ref[:, k : k + 1]
+        labels = jnp.where(lane == k, route_ref[:, k : k + 1], labels)
+        labels = jnp.where(lane == topk + k, lax.shift_right_logical(gate, 8), labels)
+        labels = jnp.where(lane == 2 * topk + k, gate & 255, labels)
+    labels = labels.astype(jnp.float32).astype(jnp.bfloat16)
+    own_ref[:rows, :width] = tok_ref[...]
+    own_ref[rows:, :width] = cot_ref[...]
+    own_ref[:rows, width:] = labels
+    own_ref[rows:, width:] = jnp.zeros_like(labels)
 
     def slab(z, d):
-        return out_ref.at[:, level[z], spot[d]]
+        return out_ref.at[level[z], spot[d]]
 
     def send(index, src, dst, peer):
         copies[index] = remote(src, dst, sems, index, peer)
@@ -183,7 +202,7 @@
     def corners(z):
         for d, at, half, peer in ((1, x_at, 0, along_y), (2, y_at, 1, along_x)):
             arrived(at + z)
-            part = out_ref.at[half, level[z], spot[d]]
+            part = slab(z, d).at[:, pl.ds(half * middle, columns - middle if half else middle)]
             send(diag_at + 2 * z + half, part, part, peer)
             send(sib_at + 4 * z + d, slab(z, d), slab(z, d), sibling)
 
@@ -218,21 +237,23 @@
     keep.wait()
 
 
-def gather_all(own):
-    halves, rows, columns = own.shape
+def gather_all(tokens, cotangent, routes, gates):
+    rows, width = tokens.shape
+    columns = width + LANES
     experts, groups = lax.axis_size("expert"), lax.axis_size("dp")
     return pl.pallas_call(
         gather_kernel,
-        out_shape=jax.ShapeDtypeStruct((halves, experts, groups, rows, columns), own.dtype),
-        in_specs=[pl.BlockSpec(memory_space=pl.ANY)],
+        out_shape=jax.ShapeDtypeStruct((experts, groups, 2 * rows, columns), tokens.dtype),
+        in_specs=[pl.BlockSpec(memory_space=pltpu.VMEM)] * 4,
         out_specs=pl.BlockSpec(memory_space=pl.ANY),
         scratch_shapes=[
+            pltpu.VMEM((2 * rows, columns), tokens.dtype),
             pltpu.SemaphoreType.DMA,
             pltpu.SemaphoreType.DMA((36,)),
             pltpu.SemaphoreType.DMA((36,)),
         ],
         compiler_params=pltpu.CompilerParams(collective_id=0, has_side_effects=True),
-    )(own)
+    )(tokens, cotangent, routes, gates)
 
 
 def return_kernel(
@@ -256,7 +277,8 @@
     for c in range(CHUNKS):
         for r in (3, 1, 2):
             send(c * step + r, parts_ref.at[mates[r] * CHUNKS + c], first.at[c, r], (me, mates[r]))
-    for c in range(CHUNKS):
+
+    def back(c):
         total = parts_ref[group * CHUNKS + c].astype(jnp.float32)
         for r in (1, 2, 3):
             copies[c * step + r].wait_recv()
@@ -268,7 +290,8 @@
         for m in (4, 5, 3, 6, 2, 7, 1):
             send(c * step + 3 + m, second.at[c, others[m]], second_in.at[c, me], (others[m], group))
         second_in[c, me] = second[c, me]
-    for c in range(CHUNKS):
+
+    def join(c):
         for m in range(1, experts):
             copies[c * step + 3 + m].wait_recv()
         total = jnp.zeros((place_ref.shape[1], second.shape[3]), jnp.float32)
@@ -283,6 +306,12 @@
         for r in (3, 1, 2):
             send(c * step + 2 + experts + r, third.at[c, mates[r]], third_in.at[c, group], (me, mates[r]))
         third_in[c, group] = third[c, group]
+
+    for c in range(CHUNKS + LAG):
+        if c < CHUNKS:
+            back(c)
+        if c >= LAG:
+            join(c - LAG)
     for c in range(CHUNKS):
         for r in (1, 2, 3):
             copies[c * step + 2 + experts + r].wait_recv()
@@ -328,7 +357,6 @@
     rows_here, width = tokens.shape[2:]
     topk = routes.shape[3]
     units = w_gate.shape[2]
-    half = width // 2
     expert_count = lax.axis_size("expert")
     group_count = lax.axis_size("dp")
     column_tok = group_count * rows_here
@@ -338,22 +366,12 @@
     expert_iota = jnp.arange(expert_count, dtype=jnp.int32)
     partner = jnp.sum(jnp.where(expert_iota == self_index, matching, 0))
     flipped = partner != self_index
-    gate_here = gates[0, 0]
-    labels = jnp.concatenate([routes[0, 0], gate_here // 256, gate_here % 256], axis=1)
-    labels = jnp.pad(labels, ((0, rows_here), (0, LANES - 3 * topk))).astype(jnp.bfloat16)
-    body = jnp.concatenate([tokens[0, 0], cotangent[0, 0]], axis=0)
-    own = jnp.stack(
-        [
-            jnp.concatenate([body[:, :half], labels], axis=1),
-            jnp.concatenate([body[:, half:], labels], axis=1),
-        ]
-    )
-    everything = gather_all(own)
-    labels = everything[0, :, :, :rows_here, half : half + 3 * topk].astype(jnp.int32)
+    everything = gather_all(tokens[0, 0], cotangent[0, 0], routes[0, 0], gates[0, 0])
+    labels = everything[:, :, :rows_here, width : width + 3 * topk].astype(jnp.int32)
     labels = labels.reshape(expert_count, column_tok, 3, topk)
     route = labels[:, :, 0]
     gate = labels[:, :, 1] * 256 + labels[:, :, 2]
-    rows_all = everything.reshape(2, expert_count * group_count * 2 * rows_here, half + LANES)
+    rows_all = everything.reshape(expert_count * group_count * 2 * rows_here, width + LANES)
 
     def ranked(expert):
         hit = jnp.any(route == expert, axis=2)
@@ -371,21 +389,15 @@
         iota = jnp.arange(slot_count, dtype=jnp.int32)[:, None]
         pick = jnp.concatenate([from_tok[None] == iota, from_cot[None] == iota], axis=0)
         pick = pick.astype(jnp.bfloat16)
-        return [
-            jnp.dot(pick, rows_all[i], preferred_element_type=jnp.float32)[:, :half].astype(
-                jnp.bfloat16
-            )
-            for i in range(2)
-        ]
+        both = jnp.dot(pick, rows_all, preferred_element_type=jnp.float32).astype(jnp.bfloat16)
+        return both[:slot_count, :width], both[slot_count:, :width]
 
     weight = jnp.sum(jnp.where(route == self_index, gate, 0), axis=2).reshape(-1)
     own_slot = ranked(self_index).reshape(-1)
     slot_iota = jnp.arange(slot_count, dtype=jnp.int32)[:, None]
     weight = jnp.sum(jnp.where(own_slot[None] == slot_iota, weight[None], 0), axis=1)
     weight = (weight.astype(jnp.float32) / 65536.0)[:, None]
-    mine = picked(self_index)
-    rows_in = jnp.concatenate([block[:slot_count] for block in mine], axis=1)
-    rows_cot = jnp.concatenate([block[slot_count:] for block in mine], axis=1)
+    rows_in, rows_cot = picked(self_index)
     rows_cot = (rows_cot.astype(jnp.float32) * weight).astype(jnp.bfloat16)
     gate_act = jnp.dot(rows_in, w_gate[0], preferred_element_type=jnp.float32)
     up_act = jnp.dot(rows_in, w_up[0], preferred_element_type=jnp.float32)
@@ -422,9 +434,7 @@
         parts, packed, jnp.asarray(widen, jnp.bfloat16), place, rows_out
     )
     chosen = jnp.where(flipped, swapped, packed)
-    theirs = picked(partner)
-    their_rows = jnp.concatenate([block[:slot_count] for block in theirs], axis=1)
-    their_cot = jnp.concatenate([block[slot_count:] for block in theirs], axis=1)
+    their_rows, their_cot = picked(partner)
     grad_gate = contract_rows(their_rows, chosen[:, :units]).astype(jnp.bfloat16)
     grad_up = contract_rows(their_rows, chosen[:, units : 2 * units]).astype(jnp.bfloat16)
     grad_down = contract_rows(chosen[:, 2 * units :], their_cot).astype(jnp.bfloat16)

time: 152 us -> 147 us (0.967)
  matrix products: 25.3 us -> 38.5 us
  local copies, waits for them, and re-layouts: 17.5 us -> 6.96 us
  other arithmetic: 7.93 us -> 3.69 us
  Pallas kernels: 99.2 us -> 96.2 us
    slice x5 -> x0, local copies, waits for them, and re-layouts: 10.2 us -> none  [the longest x1 9.65 us: picked(): rows_all[i]]
    dot_general x4 -> x2, matrix products: 10.5 us -> 17.5 us  [picked(): jnp.dot(pick, rows_all, preferred_element_type=jnp.float32)]
    pallas_call x1, Pallas kernels: 43.1 us -> 39.7 us  [return_all(): pl.pallas_call(return_kernel, out_shape=(jax.ShapeDtypeStruct((rows_out,...]
    dot_general x3, matrix products: 4.27 us -> 6.91 us  [contract_units(): lax.dot_general(left, right, (((1,), (1,)), ((), ())), preferred_element_...]
    unnamed x16, local copies, waits for them, and re-layouts: 3.97 us -> 1.77 us
    another operation x3 -> x0, other arithmetic: 1.8 us -> none  [the longest x2 1.78 us: small_shards(): jnp.stack([jnp.concatenate([body[:, :half], labels], axis=1), jnp.concate...]
    dot_general x1, matrix products: 0.71 us -> 2.48 us  [small_shards(): up_act = jnp.dot(rows_in, w_up[0], preferred_element_type=jnp.float32)]
    dot_general x3, matrix products: 9.1 us -> 10.8 us  [contract_rows(): lax.dot_general(left, right, (((0,), (0,)), ((), ())), preferred_element_...]
where the time goes in v3:
time: 147 us
  Pallas kernels  96.2 us (65%)
  matrix products  38.5 us (26%)
  local copies, waits for them, and re-layouts  6.96 us (5%)
  other arithmetic  3.69 us (3%)
  between operations  1.55 us (1%)
    pallas_call x1, Pallas kernels, gather_all(): pl.pallas_call(gather_kernel, out_shape=jax.ShapeDtypeStruct((experts, gr...  56.5 us
    pallas_call x1, Pallas kernels, return_all(): pl.pallas_call(return_kernel, out_shape=(jax.ShapeDtypeStruct((rows_out,...  39.7 us
    dot_general x2, matrix products, picked(): jnp.dot(pick, rows_all, preferred_element_type=jnp.float32)  17.5 us
    dot_general x3, matrix products, contract_rows(): lax.dot_general(left, right, (((0,), (0,)), ((), ())), preferred_element_...  10.8 us
    dot_general x3, matrix products, contract_units(): lax.dot_general(left, right, (((1,), (1,)), ((), ())), preferred_element_...  6.91 us

profile of v3, /device:TPU:0, one launch (start us, length us, event | category | flops | bytes accessed | tf_op | source)
XLA Modules:
  0.0 146.9 jit_solution(5629807942636802920)
XLA Ops:
  0.6 1.4 copy.29.route_ref
  2.0 1.4 copy.30.gate_ref
  3.4 56.5 %shard_map.120 = bf16[8,4,24,7296]{3,2,1,0:T(8,128)(2,1)} custom-call(bf16[12,7168]{1,0:T(8,128)(2,1)} %bitcast.64, bf16[12,7168]{1,0:T(8,128)(2,1)} %bitcast.65, s32[12,2]{1,0:T(8,128)} %copy.29.route_ref, s32[12,2]{1,0:T(8,128)} %copy.30.gate_ref), custom_call_target="tpu_custom_call" | custom-call | tf_op jit(solution)/shard_map/pallas_call | solution.py:244
  59.8 0.9 slice_convert_fusion
  60.8 0.4 copy.31
  61.1 0.1 reshape.112
  61.3 0.1 select_reduce_fusion.1
  61.4 0.6 select_reduce_fusion.2
  62.0 0.7 fusion.33
  62.8 0.5 convert_reduce_fusion
  63.6 0.1 eq.137
  63.8 0.1 eq.133
  64.0 8.2 %convolution_convert_fusion.1 = bf16[288,7296]{1,0:T(8,128)(2,1)S(1)} fusion(bf16[768,7296]{1,0:T(8,128)(2,1)} %bitcast.59, pred[144,768]{1,0:T(8,128)(4,1)S(1)} %iota_compare_fusion.2, pred[144,768]{1,0:T(8,128)(4,1)S(1)} %iota_compare_fusion.3), kind=kOutput, calls=%fused_computation.1 | convolution fusion | flops 3229839360 | bytes 15630336 | tf_op jit(solution)/shard_map/dot_general | solution.py:392
  72.2 0.8 fusion.6
  73.0 1.3 copy-done.5
  74.5 0.1 select_reduce_fusion
  74.7 4.2 %fusion.11 = f32[144,256]{1,0:T(8,128)S(1)} fusion(bf16[1,256,7168]{2,1,0:T(8,128)(2,1)} %param.13, bf16[288,7296]{1,0:T(8,128)(2,1)} %copy-done.5, f32[144]{0:T(256)S(1)} %convert_multiply_fusion), kind=kOutput, calls=%fused_computation.18 | convolution fusion | flops 531578880 | bytes 5882432 | tf_op jit(solution)/shard_map/dot_general | solution.py:37
  78.9 2.5 %multiply_convert_fusion.2 = (bf16[144,256]{1,0:T(8,128)(2,1)S(1)}, bf16[144,256]{1,0:T(8,128)(2,1)S(1)}, bf16[144,256]{1,0:T(8,128)(2,1)S(1)}) fusion(f32[144,256]{1,0:T(8,128)S(1)} %fusion.6, f32[144]{0:T(256)S(1)} %convert_multiply_fusion, f32[144,256]{1,0:T(8,128)S(1)} %fusion.11, bf16[1,7168,256]{2,1,0:T(8,128)(2,1)S(1)} %copy-done.3, ...), kind=kOutput, calls=%fused_computation.49 | convolution fusion | flops 529108992 | bytes 6251072 | tf_op jit(solution)/shard_map/dot_general | solution.py:403
  81.3 0.2 copy-done.2
  81.5 1.3 fusion.4
  82.9 1.4 fusion.3
  84.2 0.1 copy.35
  84.6 0.2 fusion.26
  84.8 0.3 copy-done
  85.1 39.7 %shard_map.121 = (bf16[16,7168]{1,0:T(8,128)(2,1)S(1)}, bf16[144,768]{1,0:T(8,128)(2,1)S(1)}) custom-call(bf16[28,144,256]{2,1,0:T(8,128)(2,1)S(1)} %bitcast.57, bf16[144,768]{1,0:T(8,128)(2,1)S(1)} %pad_maximum_fusion.packed_ref, bf16[8,24,144]{2,1,0:T(8,128)(2,1)S(1)} %copy-done, bf16[8,64,24]{2,1,0:T(8,128)(2,1)S(1)} %bitcast.58), custom_call_target="tpu_custom_call" | custom-call | tf_op jit(solution)/shard_map/pallas_call | solution.py:333
  124.8 0.7 slice_bitcast_fusion
  125.6 0.1 eq.159
  125.8 0.1 eq.155
  126.0 9.3 %convolution_convert_fusion = bf16[288,7296]{1,0:T(8,128)(2,1)} fusion(bf16[768,7296]{1,0:T(8,128)(2,1)} %bitcast.60, pred[144,768]{1,0:T(8,128)(4,1)S(1)} %iota_compare_fusion, pred[144,768]{1,0:T(8,128)(4,1)S(1)} %iota_compare_fusion.1), kind=kOutput, calls=%fused_computation | convolution fusion | flops 3229839360 | bytes 15630336 | tf_op jit(solution)/shard_map/dot_general | solution.py:392
  136.0 4.8 %fusion = bf16[1,7168,256]{2,1,0:T(8,128)(2,1)} fusion(bf16[288,7296]{1,0:T(8,128)(2,1)} %convolution_convert_fusion, bf16[144,768]{1,0:T(8,128)(2,1)S(1)} %broadcast_select_fusion), kind=kOutput, calls=%fused_computation.6 | convolution fusion | flops 530317312 | bytes 5808128 | tf_op jit(solution)/shard_map/dot_general | solution.py:31
  140.8 3.1 %fusion.1 = bf16[1,7168,256]{2,1,0:T(8,128)(2,1)} fusion(bf16[288,7296]{1,0:T(8,128)(2,1)S(1)} %bitcast.63, bf16[144,768]{1,0:T(8,128)(2,1)S(1)} %broadcast_select_fusion), kind=kOutput, calls=%fused_computation.7 | convolution fusion | flops 530317312 | bytes 5808128 | tf_op jit(solution)/shard_map/dot_general | solution.py:31
  143.9 3.0 %fusion.2 = bf16[1,256,7168]{2,1,0:T(8,128)(2,1)} fusion(bf16[288,7296]{1,0:T(8,128)(2,1)S(1)} %bitcast.63, bf16[144,768]{1,0:T(8,128)(2,1)S(1)} %broadcast_select_fusion), kind=kOutput, calls=%fused_computation.8 | convolution fusion | flops 530317312 | bytes 5808128 | tf_op jit(solution)/shard_map/dot_general | solution.py:31
  (38 shorter events, 1.4 us)
Async XLA Ops:
  3.3 58.0 %copy-start.4 = (s32[8]{0:T(128)S(1)}, s32[8]{0:T(128)}, u32[]{:S(2)}) copy-start(s32[8]{0:T(128)} %param.16) | copy-start | bytes 100
  64.0 8.2 %copy-start.1 = (bf16[1,7168,256]{2,1,0:T(8,128)(2,1)S(1)}, bf16[1,7168,256]{2,1,0:T(8,128)(2,1)}, u32[]{:S(2)}) copy-start(bf16[1,7168,256]{2,1,0:T(8,128)(2,1)} %param.11) | copy-start | bytes 11010052
  72.2 2.1 %copy-start.5 = (bf16[288,7296]{1,0:T(8,128)(2,1)}, bf16[288,7296]{1,0:T(8,128)(2,1)S(1)}, u32[]{:S(2)}) copy-start(bf16[288,7296]{1,0:T(8,128)(2,1)S(1)} %convolution_convert_fusion.1) | copy-start | bytes 12607492
  74.5 4.3 %copy-start.3 = (bf16[1,7168,256]{2,1,0:T(8,128)(2,1)S(1)}, bf16[1,7168,256]{2,1,0:T(8,128)(2,1)}, u32[]{:S(2)}) copy-start(bf16[1,7168,256]{2,1,0:T(8,128)(2,1)} %param.12) | copy-start | bytes 11010052
  78.8 2.7 %copy-start.2 = (bf16[1,7168,256]{2,1,0:T(8,128)(2,1)S(1)}, bf16[1,7168,256]{2,1,0:T(8,128)(2,1)}, u32[]{:S(2)}) copy-start(bf16[1,7168,256]{2,1,0:T(8,128)(2,1)} %param.11) | copy-start | bytes 11010052
  84.2 0.9 copy-start
  135.9 4.9 %slice-start = ((s8[4202496]{0:T(1024)(128)(4,1)}), s8[4194304]{0:T(1024)(128)(4,1)S(1)}, s32[]{:S(2)}) async-start(s8[4202496]{0:T(1024)(128)(4,1)} %bitcast.62), calls=%async_computation | async-start | bytes 8388608
  136.0 4.8 %slice-start.1 = ((s8[4202496]{0:T(1024)(128)(4,1)}), s8[8192]{0:T(1024)(128)(4,1)S(1)}, s32[]{:S(2)}) async-start(s8[4202496]{0:T(1024)(128)(4,1)} %bitcast.62), calls=%async_computation.1 | async-start | bytes 16384

commit v4 on v3

--- a/solution.py
+++ b/solution.py
@@ -353,6 +353,93 @@
     )(parts, packed, widen, place)
 
 
+def expert_kernel(
+    tiles, pick_ref, weight_ref, rows_ref, w_gate_ref, w_up_ref, w_down_ref,
+    theirs_ref, packed_ref, parts_ref, gate_acc, up_acc, hidden_acc,
+):
+    j = pl.program_id(0)
+    slots, units = gate_acc.shape
+
+    @pl.when(j == 0)
+    def _():
+        gate_acc[...] = jnp.zeros_like(gate_acc)
+        up_acc[...] = jnp.zeros_like(up_acc)
+        hidden_acc[...] = jnp.zeros_like(hidden_acc)
+
+    @pl.when(j < tiles)
+    def _():
+        rows = rows_ref[...]
+        mine = jnp.dot(pick_ref[: 2 * slots], rows, preferred_element_type=jnp.float32)
+        theirs = jnp.dot(pick_ref[2 * slots :], rows, preferred_element_type=jnp.float32)
+        theirs_ref[...] = theirs.astype(jnp.bfloat16)
+        rows_in = mine[:slots].astype(jnp.bfloat16)
+        rows_cot = (mine[slots:] * weight_ref[...]).astype(jnp.bfloat16)
+        gate_acc[...] += jnp.dot(rows_in, w_gate_ref[...], preferred_element_type=jnp.float32)
+        up_acc[...] += jnp.dot(rows_in, w_up_ref[...], preferred_element_type=jnp.float32)
+        hidden_acc[...] += contract_units(rows_cot, w_down_ref[...])
+
+    @pl.when(j == tiles - 1)
+    def _():
+        gate_act, up_act, d_hidden = gate_acc[...], up_acc[...], hidden_acc[...]
+        sigmoid_gate = 1.0 / (1.0 + jnp.exp(-gate_act))
+        silu = gate_act * sigmoid_gate
+        d_gate = d_hidden * up_act * sigmoid_gate * (1.0 + gate_act * (1.0 - sigmoid_gate))
+        packed_ref[:, :units] = d_gate.astype(jnp.bfloat16)
+        packed_ref[:, units : 2 * units] = (d_hidden * silu).astype(jnp.bfloat16)
+        packed_ref[:, 2 * units :] = (silu * up_act * weight_ref[...]).astype(jnp.bfloat16)
+
+    @pl.when(j >= tiles)
+    def _():
+        d_gate, d_up = packed_ref[:, :units], packed_ref[:, units : 2 * units]
+        pieces, _, columns = parts_ref.shape
+        for p in range(pieces):
+            at = pl.ds(p * columns, columns)
+            share = contract_units(d_gate, w_gate_ref[at]) + contract_units(d_up, w_up_ref[at])
+            parts_ref[p] = share.astype(jnp.bfloat16)
+
+
+def expert_all(pick, weight, rows_all, w_gate, w_up, w_down, pieces):
+    slots, units = weight.shape[0], w_gate.shape[1]
+    width = w_gate.shape[0]
+    count = rows_all.shape[0]
+    tiles = CHUNKS
+    tile = width // tiles
+    columns = width // pieces
+
+    def fixed(*shape):
+        return pl.BlockSpec(shape, lambda j: (0,) * len(shape))
+
+    def ahead(j):
+        return lax.min(j, tiles - 1)
+
+    return pl.pallas_call(
+        lambda *refs: expert_kernel(tiles, *refs),
+        grid=(2 * tiles,),
+        out_shape=(
+            jax.ShapeDtypeStruct((2 * slots, width), jnp.bfloat16),
+            jax.ShapeDtypeStruct((slots, 3 * units), jnp.bfloat16),
+            jax.ShapeDtypeStruct((pieces, slots, columns), jnp.bfloat16),
+        ),
+        in_specs=[
+            fixed(*pick.shape),
+            fixed(slots, 1),
+            pl.BlockSpec((count, tile), lambda j: (0, ahead(j))),
+            pl.BlockSpec((tile, units), lambda j: (lax.rem(j, tiles), 0)),
+            pl.BlockSpec((tile, units), lambda j: (lax.rem(j, tiles), 0)),
+            pl.BlockSpec((units, tile), lambda j: (0, ahead(j))),
+        ],
+        out_specs=(
+            pl.BlockSpec((2 * slots, tile), lambda j: (0, ahead(j))),
+            fixed(slots, 3 * units),
+            pl.BlockSpec(
+                (pieces // tiles, slots, columns), lambda j: (lax.max(j - tiles, 0), 0, 0)
+            ),
+        ),
+        scratch_shapes=[pltpu.VMEM((slots, units), jnp.float32)] * 3,
+        compiler_params=pltpu.CompilerParams(vmem_limit_bytes=40 * 2**20),
+    )(pick, weight, rows_all, w_gate, w_up, w_down)
+
+
 def small_shards(tokens, cotangent, w_gate, w_up, w_down, routes, gates, matching):
     rows_here, width = tokens.shape[2:]
     topk = routes.shape[3]
@@ -388,31 +475,18 @@
         from_cot = jnp.concatenate([none, slot], axis=2).reshape(-1)
         iota = jnp.arange(slot_count, dtype=jnp.int32)[:, None]
         pick = jnp.concatenate([from_tok[None] == iota, from_cot[None] == iota], axis=0)
-        pick = pick.astype(jnp.bfloat16)
-        both = jnp.dot(pick, rows_all, preferred_element_type=jnp.float32).astype(jnp.bfloat16)
-        return both[:slot_count, :width], both[slot_count:, :width]
+        return pick.astype(jnp.bfloat16)
 
     weight = jnp.sum(jnp.where(route == self_index, gate, 0), axis=2).reshape(-1)
     own_slot = ranked(self_index).reshape(-1)
     slot_iota = jnp.arange(slot_count, dtype=jnp.int32)[:, None]
     weight = jnp.sum(jnp.where(own_slot[None] == slot_iota, weight[None], 0), axis=1)
     weight = (weight.astype(jnp.float32) / 65536.0)[:, None]
-    rows_in, rows_cot = picked(self_index)
-    rows_cot = (rows_cot.astype(jnp.float32) * weight).astype(jnp.bfloat16)
-    gate_act = jnp.dot(rows_in, w_gate[0], preferred_element_type=jnp.float32)
-    up_act = jnp.dot(rows_in, w_up[0], preferred_element_type=jnp.float32)
-    d_hidden = contract_units(rows_cot, w_down[0])
-    sigmoid_gate = jax.nn.sigmoid(gate_act)
-    hidden = (gate_act * sigmoid_gate * up_act * weight).astype(jnp.bfloat16)
-    d_gate = (d_hidden * up_act * sigmoid_gate * (1.0 + gate_act * (1.0 - sigmoid_gate))).astype(
-        jnp.bfloat16
-    )
-    d_up = (d_hidden * gate_act * sigmoid_gate).astype(jnp.bfloat16)
-    packed = jnp.concatenate([d_gate, d_up, hidden], axis=1)
+    pick = jnp.concatenate([picked(self_index), picked(partner)], axis=0)
     pieces = group_count * CHUNKS
-    partial = contract_units(d_gate, w_gate[0]) + contract_units(d_up, w_up[0])
-    parts = partial.astype(jnp.bfloat16).reshape(slot_count, pieces, width // pieces)
-    parts = parts.transpose(1, 0, 2)
+    theirs, packed, parts = expert_all(
+        pick, weight, rows_all, w_gate[0], w_up[0], w_down[0], pieces
+    )
     wide = -(-cap_col // ROW_TILE) * ROW_TILE
     widen = np.zeros((expert_count, wide, slot_count), np.float32)
     for i in range(expert_count):
@@ -434,7 +508,7 @@
         parts, packed, jnp.asarray(widen, jnp.bfloat16), place, rows_out
     )
     chosen = jnp.where(flipped, swapped, packed)
-    their_rows, their_cot = picked(partner)
+    their_rows, their_cot = theirs[:slot_count], theirs[slot_count:]
     grad_gate = contract_rows(their_rows, chosen[:, :units]).astype(jnp.bfloat16)
     grad_up = contract_rows(their_rows, chosen[:, units : 2 * units]).astype(jnp.bfloat16)
     grad_down = contract_rows(chosen[:, 2 * units :], their_cot).astype(jnp.bfloat16)

time: 147 us -> 141 us (0.959)
  matrix products: 38.5 us -> 10.8 us
  Pallas kernels: 96.2 us -> 113 us
  local copies, waits for them, and re-layouts: 6.96 us -> 11.2 us
    dot_general x7 -> x0, matrix products: 27.7 us -> none  [the longest x2 17.5 us: picked(): jnp.dot(pick, rows_all, preferred_element_type=jnp.float32)]
    pallas_call x0 -> x1, Pallas kernels: none -> 16.8 us  [expert_all(): pl.pallas_call(lambda *refs: expert_kernel(tiles, *refs), grid=(2 * tiles...]
    unnamed x16 -> x10, local copies, waits for them, and re-layouts: 1.77 us -> 6.12 us
where the time goes in v4:
time: 141 us
  Pallas kernels  113 us (80%)
  local copies, waits for them, and re-layouts  11.2 us (8%)
  matrix products  10.8 us (8%)
  other arithmetic  4.44 us (3%)
  between operations  1.46 us (1%)
    pallas_call x1, Pallas kernels, gather_all(): pl.pallas_call(gather_kernel, out_shape=jax.ShapeDtypeStruct((experts, gr...  56.5 us
    pallas_call x1, Pallas kernels, return_all(): pl.pallas_call(return_kernel, out_shape=(jax.ShapeDtypeStruct((rows_out,...  39.8 us
    pallas_call x1, Pallas kernels, expert_all(): pl.pallas_call(lambda *refs: expert_kernel(tiles, *refs), grid=(2 * tiles...  16.8 us
    dot_general x3, matrix products, contract_rows(): lax.dot_general(left, right, (((0,), (0,)), ((), ())), preferred_element_...  10.8 us
    unnamed x10, local copies, waits for them, and re-layouts  6.12 us

profile of v4, /device:TPU:0, one launch (start us, length us, event | category | flops | bytes accessed | tf_op | source)
XLA Modules:
  0.0 141.0 jit_solution(6955287393814268901)
XLA Ops:
  0.6 1.3 select_reduce_fusion.2
  1.9 1.4 copy.29.route_ref
  3.3 1.4 copy.30.gate_ref
  4.6 56.5 %shard_map.120 = bf16[8,4,24,7296]{3,2,1,0:T(8,128)(2,1)} custom-call(bf16[12,7168]{1,0:T(8,128)(2,1)} %bitcast.40, bf16[12,7168]{1,0:T(8,128)(2,1)} %bitcast.41, s32[12,2]{1,0:T(8,128)} %copy.29.route_ref, s32[12,2]{1,0:T(8,128)} %copy.30.gate_ref), custom_call_target="tpu_custom_call" | custom-call | tf_op jit(solution)/shard_map/pallas_call | solution.py:244
  61.1 0.9 slice_convert_fusion
  62.1 0.4 copy.31
  62.4 0.1 reshape.117
  62.5 0.7 fusion.15
  63.2 0.1 select_reduce_fusion.1
  63.3 0.5 convert_reduce_fusion
  64.0 0.1 reduce_or.36
  64.0 0.1 reduce_or.38
  64.1 0.1 add_select_fusion.1
  64.2 0.1 fusion.17
  64.3 0.1 eq.149
  64.5 0.1 eq.145
  64.6 0.1 eq.137
  64.8 0.1 eq.133
  65.0 0.1 add_convert_fusion.refs_0_
  65.2 0.1 select_n.47
  65.3 0.1 select_reduce_fusion
  65.5 0.1 copy.32.refs_1_
  65.6 2.0 %copy-done = bf16[1,7168,256]{2,1,0:T(8,128)(2,1)S(1)} copy-done((bf16[1,7168,256]{2,1,0:T(8,128)(2,1)S(1)}, bf16[1,7168,256]{2,1,0:T(8,128)(2,1)}, u32[]{:S(2)}) %copy-start) | copy-done | bytes 3670040
  67.6 2.0 %copy-done.1 = bf16[1,7168,256]{2,1,0:T(8,128)(2,1)S(1)} copy-done((bf16[1,7168,256]{2,1,0:T(8,128)(2,1)S(1)}, bf16[1,7168,256]{2,1,0:T(8,128)(2,1)}, u32[]{:S(2)}) %copy-start.1) | copy-done | bytes 3670040
  69.7 2.0 %copy-done.2 = bf16[1,256,7168]{2,1,0:T(8,128)(2,1)S(1)} copy-done((bf16[1,256,7168]{2,1,0:T(8,128)(2,1)S(1)}, bf16[1,256,7168]{2,1,0:T(8,128)(2,1)}, u32[]{:S(2)}) %copy-start.2) | copy-done | bytes 3670040
  71.7 16.8 %shard_map.121 = (bf16[288,7168]{1,0:T(8,128)(2,1)}, bf16[144,768]{1,0:T(8,128)(2,1)S(1)}, bf16[28,144,256]{2,1,0:T(8,128)(2,1)S(1)}) custom-call(bf16[576,768]{1,0:T(8,128)(2,1)S(1)} %add_convert_fusion.refs_0_, f32[144,1]{1,0:T(8,128)S(1)} %copy.32.refs_1_, bf16[768,7296]{1,0:T(8,128)(2,1)} %bitcast.39, bf16[7168,256]{1,0:T(8,128)(2,1)S(1)} %bitcast.35, ...), custom_call_target="tpu_custom_call" | custom-call | tf_op jit(solution)/shard_map/pallas_call | solution.py:415
  88.7 0.2 fusion.6
  88.9 39.8 %shard_map.122 = (bf16[16,7168]{1,0:T(8,128)(2,1)S(1)}, bf16[144,768]{1,0:T(8,128)(2,1)S(1)}) custom-call(bf16[28,144,256]{2,1,0:T(8,128)(2,1)S(1)} %get-tuple-element.9.parts_ref, bf16[144,768]{1,0:T(8,128)(2,1)S(1)} %get-tuple-element.10.packed_ref, bf16[8,24,144]{2,1,0:T(8,128)(2,1)S(1)} %copy-done.3, bf16[8,64,24]{2,1,0:T(8,128)(2,1)S(1)} %bitcast.38), custom_call_target="tpu_custom_call" | custom-call | tf_op jit(solution)/shard_map/pallas_call | solution.py:333
  129.4 4.7 %fusion.2 = bf16[1,256,7168]{2,1,0:T(8,128)(2,1)} fusion(bf16[288,7168]{1,0:T(8,128)(2,1)} %get-tuple-element.12, bf16[144,768]{1,0:T(8,128)(2,1)S(1)} %broadcast_select_fusion), kind=kOutput, calls=%fused_computation.5 | convolution fusion | flops 530317312 | bytes 5808128 | tf_op jit(solution)/shard_map/dot_general | solution.py:31
  134.1 3.1 %fusion.1 = bf16[1,7168,256]{2,1,0:T(8,128)(2,1)} fusion(bf16[288,7168]{1,0:T(8,128)(2,1)S(1)} %copy-done.4, bf16[144,768]{1,0:T(8,128)(2,1)S(1)} %broadcast_select_fusion), kind=kOutput, calls=%fused_computation.4 | convolution fusion | flops 530317312 | bytes 5808128 | tf_op jit(solution)/shard_map/dot_general | solution.py:31
  137.2 3.1 %fusion = bf16[1,7168,256]{2,1,0:T(8,128)(2,1)} fusion(bf16[288,7168]{1,0:T(8,128)(2,1)S(1)} %copy-done.4, bf16[144,768]{1,0:T(8,128)(2,1)S(1)} %broadcast_select_fusion), kind=kOutput, calls=%fused_computation.3 | convolution fusion | flops 530317312 | bytes 5808128 | tf_op jit(solution)/shard_map/dot_general | solution.py:31
  140.3 0.7 slice_bitcast_fusion
  (24 shorter events, 0.8 us)
Async XLA Ops:
  65.6 2.0 %copy-start = (bf16[1,7168,256]{2,1,0:T(8,128)(2,1)S(1)}, bf16[1,7168,256]{2,1,0:T(8,128)(2,1)}, u32[]{:S(2)}) copy-start(bf16[1,7168,256]{2,1,0:T(8,128)(2,1)} %param.11) | copy-start | bytes 11010052
  67.6 2.0 %copy-start.1 = (bf16[1,7168,256]{2,1,0:T(8,128)(2,1)S(1)}, bf16[1,7168,256]{2,1,0:T(8,128)(2,1)}, u32[]{:S(2)}) copy-start(bf16[1,7168,256]{2,1,0:T(8,128)(2,1)} %param.12) | copy-start | bytes 11010052
  69.7 2.0 %copy-start.2 = (bf16[1,256,7168]{2,1,0:T(8,128)(2,1)S(1)}, bf16[1,256,7168]{2,1,0:T(8,128)(2,1)}, u32[]{:S(2)}) copy-start(bf16[1,256,7168]{2,1,0:T(8,128)(2,1)} %param.13) | copy-start | bytes 11010052
  71.7 17.2 %copy-start.3 = (bf16[8,24,144]{2,1,0:T(8,128)(2,1)S(1)}, bf16[8,24,144]{2,1,0:T(8,128)(2,1)}, u32[]{:S(2)}) copy-start(bf16[8,24,144]{2,1,0:T(8,128)(2,1)} %constant.23.clone.widen_ref) | copy-start | bytes 165892
  129.4 4.8 %copy-start.4 = (bf16[288,7168]{1,0:T(8,128)(2,1)S(1)}, bf16[288,7168]{1,0:T(8,128)(2,1)}, u32[]{:S(2)}) copy-start(bf16[288,7168]{1,0:T(8,128)(2,1)} %get-tuple-element.12) | copy-start | bytes 12386308

commit v5 on v4

--- a/solution.py
+++ b/solution.py
@@ -152,7 +152,7 @@
 
 
 def gather_kernel(
-    tok_ref, cot_ref, route_ref, gate_ref, out_ref, own_ref, local_sem, send_sem, recv_sem
+    tok_ref, cot_ref, label_ref, out_ref, own_ref, local_sem, send_sem, recv_sem
 ):
     me, group = lax.axis_index("expert"), lax.axis_index("dp")
     sems = (send_sem, recv_sem)
@@ -165,12 +165,12 @@
     rows, width = tok_ref.shape
     columns = out_ref.shape[3]
     middle = width // 2
-    topk = route_ref.shape[1]
+    topk = label_ref.shape[1] // 2
     lane = lax.broadcasted_iota(jnp.int32, (rows, columns - width), 1)
     labels = jnp.zeros_like(lane)
     for k in range(topk):
-        gate = gate_ref[:, k : k + 1]
-        labels = jnp.where(lane == k, route_ref[:, k : k + 1], labels)
+        gate = label_ref[:, topk + k : topk + k + 1]
+        labels = jnp.where(lane == k, label_ref[:, k : k + 1], labels)
         labels = jnp.where(lane == topk + k, lax.shift_right_logical(gate, 8), labels)
         labels = jnp.where(lane == 2 * topk + k, gate & 255, labels)
     labels = labels.astype(jnp.float32).astype(jnp.bfloat16)
@@ -237,14 +237,14 @@
     keep.wait()
 
 
-def gather_all(tokens, cotangent, routes, gates):
+def gather_all(tokens, cotangent, labels):
     rows, width = tokens.shape
     columns = width + LANES
     experts, groups = lax.axis_size("expert"), lax.axis_size("dp")
     return pl.pallas_call(
         gather_kernel,
         out_shape=jax.ShapeDtypeStruct((experts, groups, 2 * rows, columns), tokens.dtype),
-        in_specs=[pl.BlockSpec(memory_space=pltpu.VMEM)] * 4,
+        in_specs=[pl.BlockSpec(memory_space=pltpu.VMEM)] * 3,
         out_specs=pl.BlockSpec(memory_space=pl.ANY),
         scratch_shapes=[
             pltpu.VMEM((2 * rows, columns), tokens.dtype),
@@ -253,12 +253,12 @@
             pltpu.SemaphoreType.DMA((36,)),
         ],
         compiler_params=pltpu.CompilerParams(collective_id=0, has_side_effects=True),
-    )(tokens, cotangent, routes, gates)
+    )(tokens, cotangent, labels)
 
 
 def return_kernel(
-    parts_ref, packed_ref, widen_ref, place_ref, out_ref, swapped_ref,
-    first, second, second_in, third, third_in, send_sem, recv_sem,
+    parts_ref, packed_ref, widen_ref, place_ref, pick_ref, rows_ref, out_ref, swapped_ref,
+    theirs_ref, first, second, second_in, third, third_in, held, send_sem, recv_sem, tile_sem,
 ):
     me, group = lax.axis_index("expert"), lax.axis_index("dp")
     experts = second.shape[1]
@@ -272,6 +272,20 @@
         copies[index] = remote(src, dst, sems, index, peer)
         copies[index].start()
 
+    tile = held.shape[2]
+
+    def fetch(c):
+        source = rows_ref.at[:, pl.ds(c * tile, tile)]
+        return pltpu.make_async_copy(source, held.at[c % 2], tile_sem.at[c % 2])
+
+    def pick(c):
+        fetch(c).wait()
+        if c + 1 < CHUNKS:
+            fetch(c + 1).start()
+        rows = jnp.dot(pick_ref[...], held[c % 2], preferred_element_type=jnp.float32)
+        theirs_ref[:, c * tile : (c + 1) * tile] = rows.astype(jnp.bfloat16)
+
+    fetch(0).start()
     greet([(me, mates[r]) for r in (1, 2, 3)] + [(others[m], group) for m in range(1, experts)])
     send(CHUNKS * step, packed_ref, swapped_ref, (flip(me, experts // 2), group))
     for c in range(CHUNKS):
@@ -309,6 +323,7 @@
 
     for c in range(CHUNKS + LAG):
         if c < CHUNKS:
+            pick(c)
             back(c)
         if c >= LAG:
             join(c - LAG)
@@ -324,7 +339,7 @@
         copy.wait_send()
 
 
-def return_all(parts, packed, widen, place, rows_out):
+def return_all(parts, packed, widen, place, pick, rows_all, rows_out):
     pieces, slots, columns = parts.shape
     experts, wide = widen.shape[:2]
     groups = pieces // CHUNKS
@@ -335,27 +350,30 @@
         out_shape=(
             jax.ShapeDtypeStruct((rows_out, pieces * columns), jnp.bfloat16),
             jax.ShapeDtypeStruct(packed.shape, packed.dtype),
-        ),
-        in_specs=[vmem] * 4,
-        out_specs=(vmem, vmem),
+            jax.ShapeDtypeStruct((pick.shape[0], pieces * columns), jnp.bfloat16),
+        ),
+        in_specs=[vmem] * 5 + [pl.BlockSpec(memory_space=pl.ANY)],
+        out_specs=(vmem, vmem, vmem),
         scratch_shapes=[
             pltpu.VMEM((CHUNKS, 4, slots, columns), jnp.bfloat16),
             pltpu.VMEM((CHUNKS, experts, wide, columns), jnp.bfloat16),
             pltpu.VMEM((CHUNKS, experts, wide, columns), jnp.bfloat16),
             pltpu.VMEM((CHUNKS, groups, rows_out, columns), jnp.bfloat16),
             pltpu.VMEM((CHUNKS, groups, rows_out, columns), jnp.bfloat16),
+            pltpu.VMEM((2, rows_all.shape[0], pieces * columns // CHUNKS), jnp.bfloat16),
             pltpu.SemaphoreType.DMA((count,)),
             pltpu.SemaphoreType.DMA((count,)),
+            pltpu.SemaphoreType.DMA((2,)),
         ],
         compiler_params=pltpu.CompilerParams(
-            collective_id=1, has_side_effects=True, vmem_limit_bytes=48 * 2**20
-        ),
-    )(parts, packed, widen, place)
+            collective_id=1, has_side_effects=True, vmem_limit_bytes=60 * 2**20
+        ),
+    )(parts, packed, widen, place, pick, rows_all)
 
 
 def expert_kernel(
     tiles, pick_ref, weight_ref, rows_ref, w_gate_ref, w_up_ref, w_down_ref,
-    theirs_ref, packed_ref, parts_ref, gate_acc, up_acc, hidden_acc,
+    packed_ref, parts_ref, gate_acc, up_acc, hidden_acc,
 ):
     j = pl.program_id(0)
     slots, units = gate_acc.shape
@@ -369,9 +387,7 @@
     @pl.when(j < tiles)
     def _():
         rows = rows_ref[...]
-        mine = jnp.dot(pick_ref[: 2 * slots], rows, preferred_element_type=jnp.float32)
-        theirs = jnp.dot(pick_ref[2 * slots :], rows, preferred_element_type=jnp.float32)
-        theirs_ref[...] = theirs.astype(jnp.bfloat16)
+        mine = jnp.dot(pick_ref[...], rows, preferred_element_type=jnp.float32)
         rows_in = mine[:slots].astype(jnp.bfloat16)
         rows_cot = (mine[slots:] * weight_ref[...]).astype(jnp.bfloat16)
         gate_acc[...] += jnp.dot(rows_in, w_gate_ref[...], preferred_element_type=jnp.float32)
@@ -416,7 +432,6 @@
         lambda *refs: expert_kernel(tiles, *refs),
         grid=(2 * tiles,),
         out_shape=(
-            jax.ShapeDtypeStruct((2 * slots, width), jnp.bfloat16),
             jax.ShapeDtypeStruct((slots, 3 * units), jnp.bfloat16),
             jax.ShapeDtypeStruct((pieces, slots, columns), jnp.bfloat16),
         ),
@@ -429,14 +444,13 @@
             pl.BlockSpec((units, tile), lambda j: (0, ahead(j))),
         ],
         out_specs=(
-            pl.BlockSpec((2 * slots, tile), lambda j: (0, ahead(j))),
             fixed(slots, 3 * units),
             pl.BlockSpec(
                 (pieces // tiles, slots, columns), lambda j: (lax.max(j - tiles, 0), 0, 0)
             ),
         ),
         scratch_shapes=[pltpu.VMEM((slots, units), jnp.float32)] * 3,
-        compiler_params=pltpu.CompilerParams(vmem_limit_bytes=40 * 2**20),
+        compiler_params=pltpu.CompilerParams(vmem_limit_bytes=60 * 2**20),
     )(pick, weight, rows_all, w_gate, w_up, w_down)
 
 
@@ -453,7 +467,8 @@
     expert_iota = jnp.arange(expert_count, dtype=jnp.int32)
     partner = jnp.sum(jnp.where(expert_iota == self_index, matching, 0))
     flipped = partner != self_index
-    everything = gather_all(tokens[0, 0], cotangent[0, 0], routes[0, 0], gates[0, 0])
+    labels = jnp.concatenate([routes[0, 0], gates[0, 0]], axis=1)
+    everything = gather_all(tokens[0, 0], cotangent[0, 0], labels)
     labels = everything[:, :, :rows_here, width : width + 3 * topk].astype(jnp.int32)
     labels = labels.reshape(expert_count, column_tok, 3, topk)
     route = labels[:, :, 0]
@@ -482,10 +497,9 @@
     slot_iota = jnp.arange(slot_count, dtype=jnp.int32)[:, None]
     weight = jnp.sum(jnp.where(own_slot[None] == slot_iota, weight[None], 0), axis=1)
     weight = (weight.astype(jnp.float32) / 65536.0)[:, None]
-    pick = jnp.concatenate([picked(self_index), picked(partner)], axis=0)
     pieces = group_count * CHUNKS
-    theirs, packed, parts = expert_all(
-        pick, weight, rows_all, w_gate[0], w_up[0], w_down[0], pieces
+    packed, parts = expert_all(
+        picked(self_index), weight, rows_all, w_gate[0], w_up[0], w_down[0], pieces
     )
     wide = -(-cap_col // ROW_TILE) * ROW_TILE
     widen = np.zeros((expert_count, wide, slot_count), np.float32)
@@ -504,8 +518,9 @@
     place = place.reshape(expert_count, group_count, rows_here, wide)
     place = jnp.pad(place, ((0, 0), (0, 0), (0, rows_out - rows_here), (0, 0)))
     place = place.reshape(expert_count, group_count * rows_out, wide).astype(jnp.bfloat16)
-    total, swapped = return_all(
-        parts, packed, jnp.asarray(widen, jnp.bfloat16), place, rows_out
+    widen = jnp.asarray(widen, jnp.bfloat16)
+    total, swapped, theirs = return_all(
+        parts, packed, widen, place, picked(partner), rows_all, rows_out
     )
     chosen = jnp.where(flipped, swapped, packed)
     their_rows, their_cot = theirs[:slot_count], theirs[slot_count:]

time: 141 us -> 145 us (1.028)
  local copies, waits for them, and re-layouts: 11.2 us -> 4.89 us
  Pallas kernels: 113 us -> 119 us
  other arithmetic: 4.44 us -> 8.33 us
    unnamed x10 -> x4, local copies, waits for them, and re-layouts: 6.12 us -> 0.01 us
    pallas_call x1, Pallas kernels: 39.8 us -> 43.8 us  [return_all(): pl.pallas_call(return_kernel, out_shape=(jax.ShapeDtypeStruct((rows_out,...]
    squeeze x2 -> x0, local copies, waits for them, and re-layouts: 2.72 us -> none  [the longest x1 1.36 us: small_shards(): routes[0, 0]]
    pallas_call x1, Pallas kernels: 16.8 us -> 19 us  [expert_all(): pl.pallas_call(lambda *refs: expert_kernel(tiles, *refs), grid=(2 * tiles...]
    convert_element_type x0 -> x2, other arithmetic: none -> 1.59 us  [picked(): return pick.astype(jnp.bfloat16)]
where the time goes in v5:
time: 145 us
  Pallas kernels  119 us (82%)
  matrix products  10.7 us (7%)
  other arithmetic  8.33 us (6%)
  local copies, waits for them, and re-layouts  4.89 us (3%)
    pallas_call x1, Pallas kernels, gather_all(): pl.pallas_call(gather_kernel, out_shape=jax.ShapeDtypeStruct((experts, gr...  56.5 us
    pallas_call x1, Pallas kernels, return_all(): pl.pallas_call(return_kernel, out_shape=(jax.ShapeDtypeStruct((rows_out,...  43.8 us
    pallas_call x1, Pallas kernels, expert_all(): pl.pallas_call(lambda *refs: expert_kernel(tiles, *refs), grid=(2 * tiles...  19 us
    dot_general x3, matrix products, contract_rows(): lax.dot_general(left, right, (((0,), (0,)), ((), ())), preferred_element_...  10.7 us

profile of v5, /device:TPU:0, one launch (start us, length us, event | category | flops | bytes accessed | tf_op | source)
XLA Modules:
  0.0 144.6 jit_solution(4946042227058881484)
XLA Ops:
  0.6 1.3 select_reduce_fusion.2
  2.6 0.7 pad_add_fusion
  3.3 0.7 copy.27.label_ref
  4.0 56.5 %shard_map.120 = bf16[8,4,24,7296]{3,2,1,0:T(8,128)(2,1)} custom-call(bf16[12,7168]{1,0:T(8,128)(2,1)} %bitcast.41, bf16[12,7168]{1,0:T(8,128)(2,1)} %bitcast.42, s32[12,4]{1,0:T(8,128)} %copy.27.label_ref), custom_call_target="tpu_custom_call" | custom-call | tf_op jit(solution)/shard_map/pallas_call | solution.py:244
  60.5 0.9 slice_convert_fusion
  61.4 0.4 copy.28
  61.8 0.1 reshape.117
  61.9 0.1 select_reduce_fusion.1
  62.0 0.7 fusion.13
  62.7 0.1 broadcast_in_dim.49
  62.8 0.1 reduce_or.36
  62.8 0.1 and.31
  62.9 0.1 reduce_or.39
  63.0 0.5 convert_reduce_fusion
  63.6 0.1 select_n.45
  63.6 0.1 select_reduce_fusion
  64.2 0.1 eq.155
  64.3 0.1 eq.159
  64.5 0.1 eq.133
  64.5 0.1 eq.137
  64.6 0.2 fusion.6
  64.9 0.7 pad_convert_fusion
  65.5 0.7 copy.29.refs_1_
  66.5 0.8 add_convert_fusion.1.pick_ref
  67.3 0.8 add_convert_fusion.refs_0_
  68.1 19.0 %shard_map.121 = (bf16[144,768]{1,0:T(8,128)(2,1)}, bf16[28,144,256]{2,1,0:T(8,128)(2,1)}) custom-call(bf16[288,768]{1,0:T(8,128)(2,1)} %add_convert_fusion.refs_0_, f32[144,1]{1,0:T(8,128)} %copy.29.refs_1_, bf16[768,7296]{1,0:T(8,128)(2,1)} %bitcast.35, bf16[7168,256]{1,0:T(8,128)(2,1)} %bitcast.37, bf16[7168,256]{1,0:T(8,128)(2,1)} %bitcast.38, ...), custom_call_target="tpu_custom_call" | custom-call | tf_op jit(solution)/shard_map/pallas_call | solution.py:431
  87.2 43.8 %shard_map.122 = (bf16[16,7168]{1,0:T(8,128)(2,1)}, bf16[144,768]{1,0:T(8,128)(2,1)}, bf16[288,7168]{1,0:T(8,128)(2,1)}) custom-call(bf16[28,144,256]{2,1,0:T(8,128)(2,1)} %get-tuple-element.9.parts_ref, bf16[144,768]{1,0:T(8,128)(2,1)} %get-tuple-element.10.packed_ref, bf16[8,24,144]{2,1,0:T(8,128)(2,1)} %constant.23.clone.widen_ref, ...), custom_call_target="tpu_custom_call" | custom-call | tf_op jit(solution)/shard_map/pallas_call | solution.py:348
  131.0 1.1 broadcast_select_fusion
  132.1 1.8 %slice_bitcast_fusion = bf16[1,1,12,7168]{3,2,1,0:T(8,128)(2,1)} fusion(bf16[16,7168]{1,0:T(8,128)(2,1)} %get-tuple-element.11), kind=kLoop, calls=%fused_computation.18 | loop fusion | bytes 344064 | tf_op jit(solution)/shard_map/reshape | solution.py:531
  133.9 4.6 %fusion.2 = bf16[1,256,7168]{2,1,0:T(8,128)(2,1)} fusion(bf16[288,7168]{1,0:T(8,128)(2,1)} %get-tuple-element.12, bf16[144,768]{1,0:T(8,128)(2,1)S(1)} %broadcast_select_fusion), kind=kOutput, calls=%fused_computation.5 | convolution fusion | flops 530317312 | bytes 5808128 | tf_op jit(solution)/shard_map/dot_general | solution.py:31
  138.5 3.1 %fusion.1 = bf16[1,7168,256]{2,1,0:T(8,128)(2,1)} fusion(bf16[288,7168]{1,0:T(8,128)(2,1)S(1)} %copy-done, bf16[144,768]{1,0:T(8,128)(2,1)S(1)} %broadcast_select_fusion), kind=kOutput, calls=%fused_computation.4 | convolution fusion | flops 530317312 | bytes 5808128 | tf_op jit(solution)/shard_map/dot_general | solution.py:31
  141.6 3.1 %fusion = bf16[1,7168,256]{2,1,0:T(8,128)(2,1)} fusion(bf16[288,7168]{1,0:T(8,128)(2,1)S(1)} %copy-done, bf16[144,768]{1,0:T(8,128)(2,1)S(1)} %broadcast_select_fusion), kind=kOutput, calls=%fused_computation.3 | convolution fusion | flops 530317312 | bytes 5808128 | tf_op jit(solution)/shard_map/dot_general | solution.py:31
  (20 shorter events, 0.8 us)
Async XLA Ops:
  87.2 43.8 %copy-start.1 = (bf16[144,768]{1,0:T(8,128)(2,1)S(1)}, bf16[144,768]{1,0:T(8,128)(2,1)}, u32[]{:S(2)}) copy-start(bf16[144,768]{1,0:T(8,128)(2,1)} %get-tuple-element.10.packed_ref) | copy-start | bytes 663556
  130.9 7.6 %copy-start = (bf16[288,7168]{1,0:T(8,128)(2,1)S(1)}, bf16[288,7168]{1,0:T(8,128)(2,1)}, u32[]{:S(2)}) copy-start(bf16[288,7168]{1,0:T(8,128)(2,1)} %get-tuple-element.12) | copy-start | bytes 12386308
